TPU v7x, 256 devices: a whole 4x4x8 slice. The times are simulated.
256 devices in a mesh: fsdp: 32 (over x, y, z_lo), tensor: 8 (over z_hi, core).
Axes of the slice: x: 4, y: 4, z: 8 (z_hi: 4, z_lo: 2; z = z_hi * 2 + z_lo), core: 2. Of those that a mesh axis runs over, the one named last changes fastest.
Arguments:
- activations: bfloat16 [2, 20480, 27648], P(None, 'fsdp', 'tensor'), may hold values from -6 to 6
- out_grads: bfloat16 [2, 20480, 5120], P(None, 'fsdp', 'tensor'), may hold values from -6 to 6
- in_maps: bfloat16 [2, 256, 27648], P(None, 'fsdp', 'tensor'), may hold values from -0.0390625 to 0.0390625
- out_maps: bfloat16 [2, 256, 5120], P(None, 'fsdp', 'tensor'), may hold values from -0.078125 to 0.078125
- col_scale: float32 [2, 27648], P(None, 'tensor'), may hold values from 0.3 to 3
- row_scale: float32 [2, 5120], P(None, 'tensor'), may hold values from 0.3 to 3
- white_left: float32 [2, 256, 256], replicated, may hold values from -0.375 to 0.375
- white_right: float32 [2, 256, 256], replicated, may hold values from -0.375 to 0.375
- doc_lengths: int32 [32, 4], P('fsdp'), may hold values from 1 to 320, 640 in all within a row
- queries: bfloat16 [512, 2, 256, 256], P('fsdp', None, None, 'tensor'), may hold values from -6 to 6
Outputs:
- scores: float32 [128, 512], P('fsdp', 'tensor')
Inputs may be any that keep to these rules, and one draw needn't show every extreme that they name: `doc_lengths`: each row sums to 640; each row's largest count is exactly 320.
All inputs are finite; a program needn't handle non-finite values.
Results may differ from a plain program's by a relative error of at most 0.007.
Values may be sent and summed in bfloat16 or wider, within the bound.
No kernel may reach another device: no remote copies, remote signals or barrier semaphores. Data moves between devices by JAX's collectives and lax.ppermute only.
A program may use at most 128 MiB of HBM per device.

v0:
```python
import math

import jax
import jax.numpy as jnp
from jax import lax
from jax.sharding import PartitionSpec as P


def layer_features(member, left_layer, right_layer):
    masked = member.T[:, :, None] * left_layer[None]
    count = masked.shape[0]
    width = masked.shape[2]
    stacked = masked.transpose(0, 2, 1).reshape(count * width, masked.shape[1])
    product = jnp.dot(stacked, right_layer, preferred_element_type=jnp.float32)
    return product.reshape(count, width, right_layer.shape[1])


def body(
    activations,
    out_grads,
    in_maps,
    out_maps,
    col_scale,
    row_scale,
    white_left,
    white_right,
    doc_lengths,
    queries,
):
    full_in, full_out = (
        lax.all_gather(in_maps, "fsdp", axis=1, tiled=True),
        lax.all_gather(out_maps, "fsdp", axis=1, tiled=True),
    )
    scaled_in = (full_in.astype(jnp.float32) * col_scale[:, None, :]).astype(jnp.bfloat16)
    scaled_out = (full_out.astype(jnp.float32) * row_scale[:, None, :]).astype(jnp.bfloat16)
    layer_count = activations.shape[0]
    proj_in = jnp.stack(
        [
            jnp.dot(activations[layer], scaled_in[layer].T, preferred_element_type=jnp.float32)
            for layer in range(layer_count)
        ]
    )
    proj_out = jnp.stack(
        [
            jnp.dot(out_grads[layer], scaled_out[layer].T, preferred_element_type=jnp.float32)
            for layer in range(layer_count)
        ]
    )
    part_right = jnp.einsum("ltk,lkm->ltm", proj_in, white_right, precision=lax.Precision.HIGHEST)
    part_left = jnp.einsum("lti,lji->ltj", proj_out, white_left, precision=lax.Precision.HIGHEST)
    left_sum = lax.psum(part_left, "tensor")
    right_sum = lax.psum_scatter(part_right, "tensor", scatter_dimension=2, tiled=True)
    left_half = left_sum.astype(jnp.bfloat16)
    right_half = right_sum.astype(jnp.bfloat16)
    lengths = doc_lengths[0]
    ends = jnp.cumsum(lengths)
    starts = ends - lengths
    places = jnp.arange(activations.shape[1], dtype=jnp.int32)[:, None]
    member = ((places >= starts[None, :]) & (places < ends[None, :])).astype(jnp.bfloat16)
    features = jnp.stack(
        [
            layer_features(member, left_half[layer], right_half[layer])
            for layer in range(layer_count)
        ],
        axis=1,
    )
    query_f = queries.astype(jnp.float32)
    doc_part = jnp.sum(features * features, axis=(1, 2, 3))
    query_part = jnp.sum(query_f * query_f, axis=(1, 2, 3))
    doc_total, query_total = lax.psum((doc_part, query_part), "tensor")
    count = features.shape[1] * features.shape[2] * white_right.shape[2]
    doc_unit = (features * lax.rsqrt(doc_total / count + 1e-06)[:, None, None, None]).astype(
        jnp.bfloat16
    )
    doc_unit = doc_unit.reshape(features.shape[0], -1)
    query_unit = (query_f * lax.rsqrt(query_total / count + 1e-06)[:, None, None, None]).astype(
        jnp.bfloat16
    )
    query_unit = query_unit.reshape(queries.shape[0], -1)
    factor = 1.0 / math.sqrt(count)
    product = lax.dot_general(
        doc_unit,
        lax.all_gather(query_unit, "fsdp", axis=0, tiled=True),
        (((1,), (1,)), ((), ())),
        preferred_element_type=jnp.float32,
    )
    partial_scores = product * factor
    return lax.psum_scatter(partial_scores, "tensor", scatter_dimension=1, tiled=True)


def solution(mesh):
    in_specs = (
        P(None, "fsdp", "tensor"),
        P(None, "fsdp", "tensor"),
        P(None, "fsdp", "tensor"),
        P(None, "fsdp", "tensor"),
        P(None, "tensor"),
        P(None, "tensor"),
        P(),
        P(),
        P("fsdp", None),
        P("fsdp", None, None, "tensor"),
    )
    out_specs = P("fsdp", "tensor")
    return jax.shard_map(body, mesh=mesh, in_specs=in_specs, out_specs=out_specs, check_vma=False)
```

profile of v0, /device:TPU:4, one launch (start us, length us, event | category | flops | bytes accessed | tf_op | source)
XLA Modules:
  0.0 701.0 jit_solution(260153412618391154)
XLA Ops:
  6.5 0.7 all-gather.3.cloned.1.call-update
  7.3 80.4 %all_gather.9 = bf16[2,256,640]{2,1,0:T(8,128)(2,1)S(1)} all-gather(bf16[2,8,640]{2,1,0:T(8,128)(2,1)} %param.13), channel_id=1, replica_groups=mesh['fsdp'=32,'tensor'=8] {'fsdp'}, dimensions={1}, use_global_device_ids=true | all-gather | bytes 675840 | tf_op jit(solution)/shard_map/all_gather | solution.py:32
  87.7 0.8 multiply_convert_fusion.1
  88.5 74.1 %all-gather.3.cloned.1.call-done = bf16[2,256,3456]{2,1,0:T(8,128)(2,1)} async-done(((bf16[2,8,3456]{2,1,0:T(8,128)(2,1)}), bf16[2,256,3456]{2,1,0:T(8,128)(2,1)}) %all-gather.3.cloned.1.call-update) | async-done | bytes 3538960 | tf_op jit(solution)/shard_map/all_gather | solution.py:31
  162.6 2.7 multiply_convert_fusion
  165.4 4.7 fusion.21
  170.1 1.6 fusion.18
  171.7 2.6 fusion.10
  174.4 0.5 convolution_bitcast_fusion
  174.9 0.5 convolution_bitcast_fusion.1
  175.4 2.2 fusion.6
  177.6 66.5 %all-reduce.2 = bf16[2,640,256]{2,1,0:T(8,128)(2,1)S(1)} all-reduce(f32[2,640,256]{2,1,0:T(8,128)S(1)} %fusion.6), channel_id=1, replica_groups=mesh['fsdp'=32,'tensor'=8] {'tensor'}, use_global_device_ids=true, to_apply=%region_1.0 | all-reduce | flops 327680 | bytes 1966080 | tf_op jit(solution)/shard_map/psum | solution.py:51
  244.2 0.2 copy.24
  244.4 0.2 copy.27
  244.6 0.2 copy-done.5
  244.8 0.2 reduce-window.4
  245.0 0.2 copy-done.1
  245.2 0.2 fusion.30
  245.5 0.9 convert_element_type.42
  246.4 0.5 fusion.24
  246.9 0.5 fusion.27
  247.6 14.4 %all-reduce = (f32[16]{0:T(128)S(1)}, f32[4]{0:T(128)S(1)}) all-reduce(f32[16]{0:T(128)S(1)} %fusion.30, f32[4]{0:T(128)S(1)} %get-tuple-element.10), channel_id=1, replica_groups=mesh['fsdp'=32,'tensor'=8] {'tensor'}, use_global_device_ids=true, to_apply=%region_6.7 | all-reduce | flops 20 | bytes 160 | tf_op jit(solution)/shard_map/psum | solution.py:70
  262.1 1.0 copy.29
  263.2 3.0 reshape.93
  266.2 0.2 reduce-scatter.7.cloned.1.call-start
  266.4 0.3 copy.28
  266.7 0.5 stack.30
  267.2 377.5 %all-gather.5.cloned.1.call-done = bf16[512,16384]{1,0:T(8,128)(2,1)} async-done(((bf16[16,16384]{1,0:T(8,128)(2,1)}), bf16[512,16384]{1,0:T(8,128)(2,1)}) %all-gather.5.cloned.1.call-update) | async-done | bytes 16777232 | tf_op jit(solution)/shard_map/all_gather | solution.py:83
  644.7 10.2 %convolution_multiply_fusion = f32[4,512]{1,0:T(4,128)S(1)} fusion(bf16[512,16384]{1,0:T(8,128)(2,1)} %all-gather.5.cloned.1.call-done, f32[4,16384]{1,0:T(4,128)S(1)} %stack.30, f32[4]{0:T(128)S(1)} %add_rsqrt_fusion.1), kind=kOutput, calls=%fused_computation.30 | convolution fusion | flops 67241984 | bytes 17047568 | tf_op jit(solution)/shard_map/dot_general | solution.py:81
  654.9 0.9 copy.33
  655.8 37.3 %reduce-scatter.7.cloned.1.call-done = f32[64,4]{1,0:T(8,128)} async-done(((f32[512,4]{1,0:T(8,128)}), f32[64,4]{1,0:T(8,128)}) %reduce-scatter.7.cloned.1.call-update) | async-done | bytes 1040
  693.1 1.4 copy.34
  (31 shorter events, 0.7 us)
Async XLA Ops:
  6.5 165.2 %copy-start = (f32[2,256,256]{2,1,0:T(8,128)S(1)}, f32[2,256,256]{2,1,0:T(8,128)}, u32[]{:S(2)}) copy-start(f32[2,256,256]{2,1,0:T(8,128)} %param.17) | copy-start | bytes 1572868
  6.5 156.1 %copy-start.4 = (f32[2,3456]{1,0:T(2,128)S(1)}, f32[2,3456]{1,0:T(2,128)}, u32[]{:S(2)}) copy-start(f32[2,3456]{1,0:T(2,128)} %param.14) | copy-start | bytes 82948
  6.5 156.1 %all-gather.3.cloned.1.call-start = ((), (), s32[]{:S(2)}) async-start(), calls=%async_computation.2 | async-start | bytes 3649536 | tf_op jit(solution)/shard_map/all_gather | solution.py:31
  7.3 238.2 %reduce-scatter.5.cloned.1.call-start = ((), (), s32[]{:S(2)}) async-start(), calls=%async_computation.3 | async-start | bytes 1474560 | tf_op jit(solution)/shard_map/reduce_scatter | solution.py:52
  162.6 7.4 %slice-start = ((s8[8847360]{0:T(1024)(128)(4,1)}), s8[4194304]{0:T(1024)(128)(4,1)S(1)}, s32[]{:S(2)}) async-start(s8[8847360]{0:T(1024)(128)(4,1)} %bitcast.88), calls=%async_computation.6 | async-start | bytes 8388608
  162.6 7.4 %slice-start.1 = ((s8[8847360]{0:T(1024)(128)(4,1)}), s8[4194304]{0:T(1024)(128)(4,1)S(1)}, s32[]{:S(2)}) async-start(s8[8847360]{0:T(1024)(128)(4,1)} %bitcast.88), calls=%async_computation.7 | async-start | bytes 8388608
  165.4 4.7 slice-start.2
  171.7 2.7 copy-start.2
  174.4 1.0 copy-start.3
  174.4 470.4 %all-gather.5.cloned.1.call-start = ((), (), s32[]{:S(2)}) async-start(), calls=%async_computation.4 | async-start | bytes 17301504 | tf_op jit(solution)/shard_map/all_gather | solution.py:83
  244.1 0.7 copy-start.5
  244.1 1.0 copy-start.1
  266.2 426.9 %reduce-scatter.7.cloned.1.call-start = ((), (), s32[]{:S(2)}) async-start(), calls=%async_computation.5 | async-start | bytes 294912
Sparse Core Ops, SparseCore 0:
  9.2 153.4 all-gather.2
  174.5 60.9 reduce-scatter.4
  266.3 378.4 all-gather.4
  655.9 37.0 reduce-scatter.6
where the time goes:
time: 701 us
  waiting for transfers between devices  490 us (70%)
  blocking collectives  161 us (23%)
  matrix products  23.2 us (3%)
  between operations  13.3 us (2%)
  local copies, waits for them, and re-layouts  8.04 us (1%)
    all_gather x1, waiting for transfers between devices, body(): lax.all_gather(query_unit, 'fsdp', axis=0, tiled=True)  377 us
    all_gather x1, blocking collectives, body(): lax.all_gather(out_maps, 'fsdp', axis=1, tiled=True)  80.4 us
    all_gather x1, waiting for transfers between devices, body(): lax.all_gather(in_maps, 'fsdp', axis=1, tiled=True)  74.1 us
    psum x1, blocking collectives, body(): left_sum = lax.psum(part_left, 'tensor')  66.5 us
    unnamed x5, waiting for transfers between devices  38 us
    psum x1, blocking collectives, body(): doc_total, query_total = lax.psum((doc_part, query_part), 'tensor')  14.4 us
  transfers between devices with their start and end apart: 4, of which 3 were waited for; matrix products, arithmetic and copies ran while one was open for 1% of the time, Pallas kernels for 0%

commit v1 on v0

v1 whole, which is shorter than its diff:
```python
import math

import jax
import jax.numpy as jnp
from jax import lax
from jax.sharding import PartitionSpec as P

F32, BF16 = jnp.float32, jnp.bfloat16
NT = (((1,), (1,)), ((), ()))


def core_swap(value):
    pairs = [(place, place ^ 1) for place in range(lax.axis_size("tensor"))]
    return lax.ppermute(value, "tensor", pairs)


def chip_shift(value, step):
    size = lax.axis_size("tensor")
    return lax.ppermute(value, "tensor", [(src, (src + 2 * step) % size) for src in range(size)])


def relative_rows(weight, core, chip):
    rows, depth = weight.shape
    parts = weight.reshape(2, 4, rows // 8, depth)
    parts = jnp.where(core == 0, parts, parts[::-1])
    doubled = jnp.concatenate([parts, parts], axis=1)
    parts = lax.dynamic_slice_in_dim(doubled, chip, 4, axis=1)
    return parts.reshape(rows, depth)


def absolute_chunks(parts, core, chip):
    two = jnp.roll(parts, 2, axis=2)
    parts = jnp.where(chip >= 2, two, parts)
    one = jnp.roll(parts, 1, axis=2)
    parts = jnp.where(chip % 2 == 1, one, parts)
    return jnp.where(core == 0, parts, parts[:, ::-1])


def tensor_sum(total):
    other = core_swap(total[:, 1].astype(BF16))
    both = total[:, 0] + other.astype(F32)
    sends = [chip_shift(both[:, step].astype(BF16), step) for step in (1, 2, 3)]
    return both[:, 0] + sends[0].astype(F32) + sends[1].astype(F32) + sends[2].astype(F32)


def body(
    activations,
    out_grads,
    in_maps,
    out_maps,
    col_scale,
    row_scale,
    white_left,
    white_right,
    doc_lengths,
    queries,
):
    layers, tokens, hidden = activations.shape
    width = out_grads.shape[2]
    owners = lax.axis_size("fsdp")
    group = lax.axis_size("tensor")
    place = lax.axis_index("tensor")
    chip, core = place // 2, place % 2
    docs = doc_lengths.shape[1]
    own_queries, _, kout, kslice = queries.shape
    kin = kslice * group
    total_queries = own_queries * owners
    count = layers * kout * kin
    pair = layers * kslice // owners

    scaled_in = (in_maps.astype(F32) * col_scale[:, None, :]).astype(BF16)
    scaled_out = (out_maps.astype(F32) * row_scale[:, None, :]).astype(BF16)
    maps = jnp.concatenate([scaled_in, scaled_out], axis=2)
    rows = maps.shape[1]
    maps = maps.reshape(layers * rows, hidden + width)
    query_f = queries.astype(F32)
    query_sq = jnp.sum(query_f * query_f, axis=(1, 2, 3))
    query_hi = lax.reduce_precision(query_sq, 8, 7)
    query_lo = query_sq - query_hi
    squares = jnp.stack([query_hi, query_lo], axis=1).astype(BF16)
    squares = jnp.pad(squares, ((0, 0), (0, 126)))
    slices = queries.transpose(0, 1, 3, 2).reshape(own_queries, owners, pair * kout)
    slices = slices.transpose(1, 0, 2)
    shared = jnp.concatenate([maps, squares], axis=1)
    shared = jnp.broadcast_to(shared[None], (owners,) + shared.shape)
    sent = jnp.concatenate([shared, slices], axis=2)
    got = lax.all_to_all(sent, "fsdp", 0, 0, tiled=True)
    base = hidden + width
    square_got = got[:, :, base : base + 2].astype(F32)
    square_got = (square_got[:, :, 0] + square_got[:, :, 1]).reshape(total_queries)
    query_got = got[:, :, base + 128 :].reshape(total_queries, pair * kout)

    rights, lefts = [], []
    for layer in range(layers):
        block = got[:, layer * rows : (layer + 1) * rows]
        full_in = block[:, :, :hidden].reshape(owners * rows, hidden)
        full_out = block[:, :, hidden:base].reshape(owners * rows, width)
        proj_in = lax.dot_general(full_in, activations[layer], NT, preferred_element_type=F32)
        proj_out = lax.dot_general(full_out, out_grads[layer], NT, preferred_element_type=F32)
        turn = white_right[layer].T.reshape(4, 2, kin // 8, kin).transpose(1, 0, 2, 3)
        turn = relative_rows(turn.reshape(kin, kin), core, chip)
        lean = relative_rows(white_left[layer], core, chip)
        rights.append(jnp.dot(turn, proj_in, precision=lax.Precision.HIGHEST))
        lefts.append(jnp.dot(lean, proj_out, precision=lax.Precision.HIGHEST))
    left = tensor_sum(jnp.stack(lefts).reshape(layers, 2, 4, kout // 8, tokens)).astype(BF16)
    right = tensor_sum(jnp.stack(rights).reshape(layers, 2, 4, kslice, tokens)).astype(BF16)
    around = [left] + [chip_shift(left, -step) for step in (1, 2, 3)]
    around = jnp.stack(around, axis=1)
    around = jnp.stack([around, core_swap(around)], axis=1)
    left_all = absolute_chunks(around, core, chip).reshape(layers, kout, tokens)

    lengths = doc_lengths[0]
    ends = jnp.cumsum(lengths)
    starts = ends - lengths
    spots = jnp.arange(tokens, dtype=jnp.int32)[None, :]
    member = ((spots >= starts[:, None]) & (spots < ends[:, None])).astype(BF16)
    features = []
    for layer in range(layers):
        masked = (right[layer][:, None, :] * member[None]).reshape(kslice * docs, tokens)
        features.append(
            lax.dot_general(masked, left_all[layer], NT, preferred_element_type=F32)
        )
    features = jnp.stack(features)
    doc_sq = jnp.sum((features * features).reshape(layers * kslice, docs, kout), axis=(0, 2))
    doc_sent = features.astype(BF16).reshape(owners, pair * docs, kout)
    doc_got = lax.all_to_all(doc_sent, "fsdp", 0, 0, tiled=True)

    doc_rows = doc_got.reshape(owners * pair * docs, kout)
    half = (jnp.arange(owners * pair * docs) // docs) % pair
    wide = jnp.concatenate(
        [jnp.where((half == one)[:, None], doc_rows, 0) for one in range(pair)], axis=1
    )
    product = lax.dot_general(wide, query_got, NT, preferred_element_type=F32)
    score_sent = product.astype(BF16).reshape(owners, pair * docs, total_queries)
    score_got = lax.all_to_all(score_sent, "fsdp", 0, 0, tiled=True)
    scores = jnp.sum(
        score_got.astype(F32).reshape(owners * pair, docs, total_queries), axis=0
    )
    final = total_queries // group
    doc_row = jnp.tile(jnp.pad(doc_sq, (0, final - docs)), group)
    last = jnp.concatenate([scores, square_got[None], doc_row[None]], axis=0)
    last = jnp.pad(last, ((0, 8 - last.shape[0]), (0, 0)))
    last = last.reshape(8, group, final).transpose(1, 0, 2)
    last = jnp.sum(lax.all_to_all(last, "tensor", 0, 0, tiled=True), axis=0)
    factor = 1.0 / math.sqrt(count)
    doc_scale = lax.rsqrt(last[docs + 1, :docs] / count + 1e-06)
    query_scale = lax.rsqrt(last[docs] / count + 1e-06)
    return last[:docs] * doc_scale[:, None] * query_scale[None, :] * factor


def solution(mesh):
    in_specs = (
        P(None, "fsdp", "tensor"),
        P(None, "fsdp", "tensor"),
        P(None, "fsdp", "tensor"),
        P(None, "fsdp", "tensor"),
        P(None, "tensor"),
        P(None, "tensor"),
        P(),
        P(),
        P("fsdp", None),
        P("fsdp", None, None, "tensor"),
    )
    out_specs = P("fsdp", "tensor")
    return jax.shard_map(body, mesh=mesh, in_specs=in_specs, out_specs=out_specs, check_vma=False)
```

time: 701 us -> 187 us (0.27)
  waiting for transfers between devices: 490 us -> 91.5 us
  blocking collectives: 161 us -> 12 us
  starting transfers between devices: 0.31 us -> 47.6 us
  between operations: 13.3 us -> 0.53 us
    all_gather x2 -> x0, waiting for transfers between devices: 452 us -> none  [the longest x1 377 us: body(): lax.all_gather(query_unit, 'fsdp', axis=0, tiled=True)]
    all_to_all x0 -> x3, waiting for transfers between devices: none -> 86 us  [the longest x1 75.4 us: body(): got = lax.all_to_all(sent, 'fsdp', 0, 0, tiled=True)]
    psum x2 -> x0, blocking collectives: 80.9 us -> none  [the longest x1 66.5 us: body(): left_sum = lax.psum(part_left, 'tensor')]
    all_gather x1 -> x0, blocking collectives: 80.4 us -> none  [body(): lax.all_gather(out_maps, 'fsdp', axis=1, tiled=True)]
    unnamed x5 -> x0, waiting for transfers between devices: 38 us -> none
    ppermute x0 -> x12, starting transfers between devices: none -> 24.3 us  [the longest x9 23.5 us: chip_shift(): lax.ppermute(value, 'tensor', [(src, (src + 2 * step) % size) for src in...]
    all_to_all x0 -> x3, starting transfers between devices: none -> 23.3 us  [the longest x1 9.13 us: body(): got = lax.all_to_all(sent, 'fsdp', 0, 0, tiled=True)]
    all_to_all x0 -> x1, blocking collectives: none -> 12 us  [body(): last = jnp.sum(lax.all_to_all(last, 'tensor', 0, 0, tiled=True), axis=0)]
  transfers between devices with their start and end apart: 4 -> 15, of which waited for: 3 -> 7; matrix products, arithmetic and copies ran while one was open for 1% -> 8% of each run, Pallas kernels for 0% -> 0%
where the time goes in v1:
time: 187 us; the launch traced here: 183 us
  waiting for transfers between devices  91.5 us (49%)
  starting transfers between devices  47.6 us (25%)
  matrix products  16.6 us (9%)
  blocking collectives  12 us (6%)
  other arithmetic  10.5 us (6%)
  local copies, waits for them, and re-layouts  4.83 us (3%)
    all_to_all x1, waiting for transfers between devices, body(): got = lax.all_to_all(sent, 'fsdp', 0, 0, tiled=True)  75.4 us
    ppermute x9, starting transfers between devices, chip_shift(): lax.ppermute(value, 'tensor', [(src, (src + 2 * step) % size) for src in...  23.5 us
    all_to_all x1, blocking collectives, body(): last = jnp.sum(lax.all_to_all(last, 'tensor', 0, 0, tiled=True), axis=0)  12 us
    all_to_all x1, starting transfers between devices, body(): got = lax.all_to_all(sent, 'fsdp', 0, 0, tiled=True)  9.13 us
    dot_general x2, matrix products, body(): lax.dot_general(full_in, activations[layer], NT, preferred_element_type=F32)  8.81 us
    all_to_all x1, starting transfers between devices, body(): doc_got = lax.all_to_all(doc_sent, 'fsdp', 0, 0, tiled=True)  7.89 us
    all_to_all x1, starting transfers between devices, body(): score_got = lax.all_to_all(score_sent, 'fsdp', 0, 0, tiled=True)  6.28 us
    all_to_all x1, waiting for transfers between devices, body(): score_got = lax.all_to_all(score_sent, 'fsdp', 0, 0, tiled=True)  5.34 us
  transfers between devices with their start and end apart: 15, of which 7 were waited for; matrix products, arithmetic and copies ran while one was open for 8% of the time, Pallas kernels for 0%

profile of v1, /device:TPU:4, one launch (start us, length us, event | category | flops | bytes accessed | tf_op | source)
XLA Modules:
  0.0 183.5 jit_solution(16091733229377486353)
XLA Ops:
  0.0 1.3 multiply_reduce_fusion
  1.3 1.2 reshape.269
  3.6 0.9 multiply_convert_fusion
  4.9 2.6 %pad_maximum_fusion = bf16[32,16,4736]{2,1,0:T(8,128)(2,1)} fusion(bf16[32,16,512]{2,1,0:T(8,128)(2,1)S(1)} %copy.80, bf16[32,16,4224]{2,1,0:T(8,128)(2,1)S(1)} %broadcast_in_dim.21), kind=kLoop, calls=%fused_computation | loop fusion | flops 9699328 | bytes 9699328 | tf_op jit(solution)/shard_map/concatenate | solution.py:86
  7.5 9.1 %all-to-all-start = ((bf16[32,16,4736]{2,1,0:T(8,128)(2,1)}), bf16[32,16,4736]{2,1,0:T(8,128)(2,1)}, u32[]{:S(2)}, u32[]{:S(2)}) async-start(bf16[32,16,4736]{2,1,0:T(8,128)(2,1)} %pad_maximum_fusion), calls=%async_computation | async-start | bytes 9699328 | tf_op jit(solution)/shard_map/all_to_all | solution.py:87
  17.5 75.4 %all-to-all-done = bf16[32,16,4736]{2,1,0:T(8,128)(2,1)} async-done(((bf16[32,16,4736]{2,1,0:T(8,128)(2,1)}), bf16[32,16,4736]{2,1,0:T(8,128)(2,1)}, u32[]{:S(2)}, u32[]{:S(2)}) %all-to-all-start) | async-done | bytes 4849696 | tf_op jit(solution)/shard_map/all_to_all | solution.py:87
  92.9 1.4 convolution_bitcast_fusion.1
  94.4 0.8 convolution_bitcast_fusion
  95.2 1.4 convolution_bitcast_fusion.3
  96.6 0.8 convolution_bitcast_fusion.2
  97.6 4.4 %fusion.9 = f32[256,640,1,1]{1,0,3,2:T(8,128)S(1)} fusion(bf16[2,640,3456]{2,1,0:T(8,128)(2,1)} %param.10, bf16[32,16,4736]{2,1,0:T(8,128)(2,1)} %all-to-all-done), kind=kOutput, calls=%fused_computation.14 | convolution fusion | flops 1132462080 | bytes 6848512 | tf_op jit(solution)/shard_map/dot_general | solution.py:98
  102.0 4.4 %fusion.6 = f32[256,640,1,1]{1,0,3,2:T(8,128)S(1)} fusion(bf16[2,640,3456]{2,1,0:T(8,128)(2,1)} %param.10, bf16[32,16,4736]{2,1,0:T(8,128)(2,1)} %all-to-all-done), kind=kOutput, calls=%fused_computation.13 | convolution fusion | flops 1132462080 | bytes 6848512 | tf_op jit(solution)/shard_map/dot_general | solution.py:98
  106.5 0.8 convolution_bitcast_fusion.4
  107.3 0.8 convolution_bitcast_fusion.5
  108.9 5.5 %collective-permute-start.7 = (bf16[2,32,640]{2,1,0:T(8,128)(2,1)S(1)}, bf16[2,32,640]{2,1,0:T(8,128)(2,1)S(1)}, u32[]{:S(2)}, u32[]{:S(2)}) collective-permute-start(bf16[2,32,640]{2,1,0:T(8,128)(2,1)S(1)} %get-tuple-element.20), channel_id=1, source_target_pairs={{0,6},{1,7},{2,0},{3,1},{4,2},{5,3},{6,4},{7,5},{8,14},{9,15},{10,... | collective-permute-start | bytes 245768 | tf_op jit(solution)/shard_map/ppermute | solution.py:19
  114.4 1.5 collective-permute-start.6
  115.9 2.4 %collective-permute-start.5 = (bf16[2,32,640]{2,1,0:T(8,128)(2,1)S(1)}, bf16[2,32,640]{2,1,0:T(8,128)(2,1)S(1)}, u32[]{:S(2)}, u32[]{:S(2)}) collective-permute-start(bf16[2,32,640]{2,1,0:T(8,128)(2,1)S(1)} %get-tuple-element.19), channel_id=1, source_target_pairs={{0,2},{1,3},{2,4},{3,5},{4,6},{5,7},{6,0},{7,1},{8,10},{9,11},{10,... | collective-permute-start | bytes 245768 | tf_op jit(solution)/shard_map/ppermute | solution.py:19
  118.4 2.0 %collective-permute-start.3 = (bf16[2,32,640]{2,1,0:T(8,128)(2,1)S(1)}, bf16[2,32,640]{2,1,0:T(8,128)(2,1)S(1)}, u32[]{:S(2)}, u32[]{:S(2)}) collective-permute-start(bf16[2,32,640]{2,1,0:T(8,128)(2,1)S(1)} %get-tuple-element.23), channel_id=1, source_target_pairs={{0,6},{1,7},{2,0},{3,1},{4,2},{5,3},{6,4},{7,5},{8,14},{9,15},{10,... | collective-permute-start | bytes 245768 | tf_op jit(solution)/shard_map/ppermute | solution.py:19
  120.4 4.5 %collective-permute-start.2 = (bf16[2,32,640]{2,1,0:T(8,128)(2,1)S(1)}, bf16[2,32,640]{2,1,0:T(8,128)(2,1)S(1)}, u32[]{:S(2)}, u32[]{:S(2)}) collective-permute-start(bf16[2,32,640]{2,1,0:T(8,128)(2,1)S(1)} %get-tuple-element.24), channel_id=1, source_target_pairs={{0,4},{1,5},{2,6},{3,7},{4,0},{5,1},{6,2},{7,3},{8,12},{9,13},{10,... | collective-permute-start | bytes 245768 | tf_op jit(solution)/shard_map/ppermute | solution.py:19
  125.1 1.9 %collective-permute-start.10 = (bf16[2,32,640]{2,1,0:T(8,128)(2,1)S(1)}, bf16[2,32,640]{2,1,0:T(8,128)(2,1)S(1)}, u32[]{:S(2)}, u32[]{:S(2)}) collective-permute-start(bf16[2,32,640]{2,1,0:T(8,128)(2,1)S(1)} %fusion.47), channel_id=1, source_target_pairs={{0,2},{1,3},{2,4},{3,5},{4,6},{5,7},{6,0},{7,1},{8,10},{9,11},{10,... | collective-permute-start | bytes 245768 | tf_op jit(solution)/shard_map/ppermute | solution.py:19
  127.0 4.5 %collective-permute-start.9 = (bf16[2,32,640]{2,1,0:T(8,128)(2,1)S(1)}, bf16[2,32,640]{2,1,0:T(8,128)(2,1)S(1)}, u32[]{:S(2)}, u32[]{:S(2)}) collective-permute-start(bf16[2,32,640]{2,1,0:T(8,128)(2,1)S(1)} %fusion.47), channel_id=1, source_target_pairs={{0,4},{1,5},{2,6},{3,7},{4,0},{5,1},{6,2},{7,3},{8,12},{9,13},{10,... | collective-permute-start | bytes 245768 | tf_op jit(solution)/shard_map/ppermute | solution.py:19
  131.5 1.3 collective-permute-start.8
  132.9 3.1 %collective-permute-done.9 = bf16[2,32,640]{2,1,0:T(8,128)(2,1)S(1)} collective-permute-done((bf16[2,32,640]{2,1,0:T(8,128)(2,1)S(1)}, bf16[2,32,640]{2,1,0:T(8,128)(2,1)S(1)}, u32[]{:S(2)}, u32[]{:S(2)}) %collective-permute-start.9) | collective-permute-done | bytes 81952 | tf_op jit(solution)/shard_map/ppermute | solution.py:19
  137.3 1.3 collective-permute-done.11
  140.4 7.9 %all-to-all-start.1 = ((bf16[32,8,256]{2,1,0:T(8,128)(2,1)}), bf16[32,8,256]{2,1,0:T(8,128)(2,1)S(1)}, u32[]{:S(2)}, u32[]{:S(2)}) async-start(bf16[32,8,256]{2,1,0:T(8,128)(2,1)} %bitcast.61), calls=%async_computation.1 | async-start | bytes 262144 | tf_op jit(solution)/shard_map/all_to_all | solution.py:126
  148.3 1.1 slice.202
  149.4 5.2 %all-to-all-done.1 = bf16[32,8,256]{2,1,0:T(8,128)(2,1)S(1)} async-done(((bf16[32,8,256]{2,1,0:T(8,128)(2,1)}), bf16[32,8,256]{2,1,0:T(8,128)(2,1)S(1)}, u32[]{:S(2)}, u32[]{:S(2)}) %all-to-all-start.1) | async-done | bytes 131104 | tf_op jit(solution)/shard_map/all_to_all | solution.py:126
  154.7 1.1 fusion.12
  155.8 6.3 %all-to-all-start.2 = ((bf16[32,8,512]{2,1,0:T(8,128)(2,1)}), bf16[32,8,512]{2,1,0:T(8,128)(2,1)S(1)}, u32[]{:S(2)}, u32[]{:S(2)}) async-start(bf16[32,8,512]{2,1,0:T(8,128)(2,1)} %fusion.12), calls=%async_computation.2 | async-start | bytes 524288 | tf_op jit(solution)/shard_map/all_to_all | solution.py:135
  162.1 0.9 slice_convert_fusion
  163.7 5.3 %all-to-all-done.2 = bf16[32,8,512]{2,1,0:T(8,128)(2,1)S(1)} async-done(((bf16[32,8,512]{2,1,0:T(8,128)(2,1)}), bf16[32,8,512]{2,1,0:T(8,128)(2,1)S(1)}, u32[]{:S(2)}, u32[]{:S(2)}) %all-to-all-start.2) | async-done | bytes 262176 | tf_op jit(solution)/shard_map/all_to_all | solution.py:135
  169.5 12.0 %all_to_all.20 = f32[8,1,512]{2,1,0:T(1,128)S(1)} all-to-all(f32[8,1,512]{2,1,0:T(1,128)S(1)} %reshape.291), channel_id=1, replica_groups=mesh['fsdp'=32,'tensor'=8] {'tensor'}, dimensions={0} | all-to-all | bytes 32768 | tf_op jit(solution)/shard_map/all_to_all | solution.py:144
  (87 shorter events, 9.7 us)
Async XLA Ops:
  7.5 9.2 %copy-start.3 = (s32[1,4]{1,0:T(1,128)S(1)}, s32[1,4]{1,0:T(1,128)}, u32[]{:S(2)}) copy-start(s32[1,4]{1,0:T(1,128)} %param.18) | copy-start | bytes 52
  7.5 9.4 %copy-start.1 = (f32[2,256,256]{2,1,0:T(8,128)S(1)}, f32[2,256,256]{2,1,0:T(8,128)}, u32[]{:S(2)}) copy-start(f32[2,256,256]{2,1,0:T(8,128)} %param.17) | copy-start | bytes 1572868
  7.5 9.9 %copy-start.2 = (f32[2,256,256]{2,1,0:T(8,128)S(1)}, f32[2,256,256]{2,1,0:T(8,128)}, u32[]{:S(2)}) copy-start(f32[2,256,256]{2,1,0:T(8,128)} %param.16) | copy-start | bytes 1572868
  7.5 85.4 %all-to-all-start = ((bf16[32,16,4736]{2,1,0:T(8,128)(2,1)}), bf16[32,16,4736]{2,1,0:T(8,128)(2,1)}, u32[]{:S(2)}, u32[]{:S(2)}) async-start(bf16[32,16,4736]{2,1,0:T(8,128)(2,1)} %pad_maximum_fusion), calls=%async_computation | async-start | bytes 9699328 | tf_op jit(solution)/shard_map/all_to_all | solution.py:87
  16.6 76.3 %copy-start = (bf16[2,640,640]{2,1,0:T(8,128)(2,1)S(1)}, bf16[2,640,640]{2,1,0:T(8,128)(2,1)}, u32[]{:S(2)}) copy-start(bf16[2,640,640]{2,1,0:T(8,128)(2,1)} %param.11) | copy-start | bytes 4915204
  97.5 11.3 %collective-permute-start.4 = (bf16[2,4,32,640]{3,2,1,0:T(8,128)(2,1)S(1)}, bf16[2,4,32,640]{3,2,1,0:T(8,128)(2,1)S(1)}, u32[]{:S(2)}, u32[]{:S(2)}) collective-permute-start(bf16[2,4,32,640]{3,2,1,0:T(8,128)(2,1)S(1)} %fusion.27), channel_id=1, source_target_pairs={{0,1},{1,0},{2,3},{3,2},{4,5},{5,4},{6,7},{7,6},{8,9},{9,8},{10,11... | collective-permute-start | bytes 983048 | tf_op jit(solution)/shard_map/ppermute | solution.py:14
  108.2 10.0 %collective-permute-start = (bf16[2,4,32,640]{3,2,1,0:T(8,128)(2,1)S(1)}, bf16[2,4,32,640]{3,2,1,0:T(8,128)(2,1)S(1)}, u32[]{:S(2)}, u32[]{:S(2)}) collective-permute-start(bf16[2,4,32,640]{3,2,1,0:T(8,128)(2,1)S(1)} %fusion.26), channel_id=1, source_target_pairs={{0,1},{1,0},{2,3},{3,2},{4,5},{5,4},{6,7},{7,6},{8,9},{9,8},{10,11... | collective-permute-start | bytes 983048 | tf_op jit(solution)/shard_map/ppermute | solution.py:14
  108.9 15.9 %collective-permute-start.7 = (bf16[2,32,640]{2,1,0:T(8,128)(2,1)S(1)}, bf16[2,32,640]{2,1,0:T(8,128)(2,1)S(1)}, u32[]{:S(2)}, u32[]{:S(2)}) collective-permute-start(bf16[2,32,640]{2,1,0:T(8,128)(2,1)S(1)} %get-tuple-element.20), channel_id=1, source_target_pairs={{0,6},{1,7},{2,0},{3,1},{4,2},{5,3},{6,4},{7,5},{8,14},{9,15},{10,... | collective-permute-start | bytes 245768 | tf_op jit(solution)/shard_map/ppermute | solution.py:19
  114.4 10.7 %collective-permute-start.6 = (bf16[2,32,640]{2,1,0:T(8,128)(2,1)S(1)}, bf16[2,32,640]{2,1,0:T(8,128)(2,1)S(1)}, u32[]{:S(2)}, u32[]{:S(2)}) collective-permute-start(bf16[2,32,640]{2,1,0:T(8,128)(2,1)S(1)} %get-tuple-element.21), channel_id=1, source_target_pairs={{0,4},{1,5},{2,6},{3,7},{4,0},{5,1},{6,2},{7,3},{8,12},{9,13},{10,... | collective-permute-start | bytes 245768 | tf_op jit(solution)/shard_map/ppermute | solution.py:19
  115.9 9.2 %collective-permute-start.5 = (bf16[2,32,640]{2,1,0:T(8,128)(2,1)S(1)}, bf16[2,32,640]{2,1,0:T(8,128)(2,1)S(1)}, u32[]{:S(2)}, u32[]{:S(2)}) collective-permute-start(bf16[2,32,640]{2,1,0:T(8,128)(2,1)S(1)} %get-tuple-element.19), channel_id=1, source_target_pairs={{0,2},{1,3},{2,4},{3,5},{4,6},{5,7},{6,0},{7,1},{8,10},{9,11},{10,... | collective-permute-start | bytes 245768 | tf_op jit(solution)/shard_map/ppermute | solution.py:19
  118.4 13.2 %collective-permute-start.3 = (bf16[2,32,640]{2,1,0:T(8,128)(2,1)S(1)}, bf16[2,32,640]{2,1,0:T(8,128)(2,1)S(1)}, u32[]{:S(2)}, u32[]{:S(2)}) collective-permute-start(bf16[2,32,640]{2,1,0:T(8,128)(2,1)S(1)} %get-tuple-element.23), channel_id=1, source_target_pairs={{0,6},{1,7},{2,0},{3,1},{4,2},{5,3},{6,4},{7,5},{8,14},{9,15},{10,... | collective-permute-start | bytes 245768 | tf_op jit(solution)/shard_map/ppermute | solution.py:19
  120.4 12.4 %collective-permute-start.2 = (bf16[2,32,640]{2,1,0:T(8,128)(2,1)S(1)}, bf16[2,32,640]{2,1,0:T(8,128)(2,1)S(1)}, u32[]{:S(2)}, u32[]{:S(2)}) collective-permute-start(bf16[2,32,640]{2,1,0:T(8,128)(2,1)S(1)} %get-tuple-element.24), channel_id=1, source_target_pairs={{0,4},{1,5},{2,6},{3,7},{4,0},{5,1},{6,2},{7,3},{8,12},{9,13},{10,... | collective-permute-start | bytes 245768 | tf_op jit(solution)/shard_map/ppermute | solution.py:19
  124.9 8.0 %collective-permute-start.1 = (bf16[2,32,640]{2,1,0:T(8,128)(2,1)S(1)}, bf16[2,32,640]{2,1,0:T(8,128)(2,1)S(1)}, u32[]{:S(2)}, u32[]{:S(2)}) collective-permute-start(bf16[2,32,640]{2,1,0:T(8,128)(2,1)S(1)} %get-tuple-element.22), channel_id=1, source_target_pairs={{0,2},{1,3},{2,4},{3,5},{4,6},{5,7},{6,0},{7,1},{8,10},{9,11},{10,... | collective-permute-start | bytes 245768 | tf_op jit(solution)/shard_map/ppermute | solution.py:19
  125.1 7.8 %collective-permute-start.10 = (bf16[2,32,640]{2,1,0:T(8,128)(2,1)S(1)}, bf16[2,32,640]{2,1,0:T(8,128)(2,1)S(1)}, u32[]{:S(2)}, u32[]{:S(2)}) collective-permute-start(bf16[2,32,640]{2,1,0:T(8,128)(2,1)S(1)} %fusion.47), channel_id=1, source_target_pairs={{0,2},{1,3},{2,4},{3,5},{4,6},{5,7},{6,0},{7,1},{8,10},{9,11},{10,... | collective-permute-start | bytes 245768 | tf_op jit(solution)/shard_map/ppermute | solution.py:19
  127.0 9.0 %collective-permute-start.9 = (bf16[2,32,640]{2,1,0:T(8,128)(2,1)S(1)}, bf16[2,32,640]{2,1,0:T(8,128)(2,1)S(1)}, u32[]{:S(2)}, u32[]{:S(2)}) collective-permute-start(bf16[2,32,640]{2,1,0:T(8,128)(2,1)S(1)} %fusion.47), channel_id=1, source_target_pairs={{0,4},{1,5},{2,6},{3,7},{4,0},{5,1},{6,2},{7,3},{8,12},{9,13},{10,... | collective-permute-start | bytes 245768 | tf_op jit(solution)/shard_map/ppermute | solution.py:19
  131.5 5.3 %collective-permute-start.8 = (bf16[2,32,640]{2,1,0:T(8,128)(2,1)S(1)}, bf16[2,32,640]{2,1,0:T(8,128)(2,1)S(1)}, u32[]{:S(2)}, u32[]{:S(2)}) collective-permute-start(bf16[2,32,640]{2,1,0:T(8,128)(2,1)S(1)} %fusion.47), channel_id=1, source_target_pairs={{0,6},{1,7},{2,0},{3,1},{4,2},{5,3},{6,4},{7,5},{8,14},{9,15},{10,... | collective-permute-start | bytes 245768 | tf_op jit(solution)/shard_map/ppermute | solution.py:19
  136.9 1.7 collective-permute-start.11
  140.4 14.2 %all-to-all-start.1 = ((bf16[32,8,256]{2,1,0:T(8,128)(2,1)}), bf16[32,8,256]{2,1,0:T(8,128)(2,1)S(1)}, u32[]{:S(2)}, u32[]{:S(2)}) async-start(bf16[32,8,256]{2,1,0:T(8,128)(2,1)} %bitcast.61), calls=%async_computation.1 | async-start | bytes 262144 | tf_op jit(solution)/shard_map/all_to_all | solution.py:126
  155.8 13.2 %all-to-all-start.2 = ((bf16[32,8,512]{2,1,0:T(8,128)(2,1)}), bf16[32,8,512]{2,1,0:T(8,128)(2,1)S(1)}, u32[]{:S(2)}, u32[]{:S(2)}) async-start(bf16[32,8,512]{2,1,0:T(8,128)(2,1)} %fusion.12), calls=%async_computation.2 | async-start | bytes 524288 | tf_op jit(solution)/shard_map/all_to_all | solution.py:135

commit v2 on v1

v2 whole, which is shorter than its diff:
```python
import math

import jax
import jax.numpy as jnp
from jax import lax
from jax.sharding import PartitionSpec as P

F32, BF16 = jnp.float32, jnp.bfloat16
NT = (((1,), (1,)), ((), ()))

MASKS = {"z": 1, "y1": 2, "y3": 6, "x1": 8, "x3": 24}
ORDERS = (
    ("x1", "x3", "y1", "y3"),
    ("x3", "x1", "y3", "y1"),
    ("y1", "y3", "x1", "x3"),
    ("y3", "y1", "x3", "x1"),
)

COMMON = ("x3", "x1", "y3", "y1")


def held_masks(order):
    masks = [0]
    for name in ("z",) + order:
        masks = masks + [mask ^ MASKS[name] for mask in masks]
    return masks


def core_swap(value):
    pairs = [(place, place ^ 1) for place in range(lax.axis_size("tensor"))]
    return lax.ppermute(value, "tensor", pairs)


def chip_shift(value, step):
    size = lax.axis_size("tensor")
    return lax.ppermute(value, "tensor", [(src, (src + 2 * step) % size) for src in range(size)])


def owner_swap(value, step):
    mask = MASKS[step]
    pairs = [(place, place ^ mask) for place in range(lax.axis_size("fsdp"))]
    return lax.ppermute(value, "fsdp", pairs)


def after(value, *others):
    return lax.optimization_barrier((value,) + others)[0]


def tree_gather(block):
    tiles = block.shape[1] // 128
    cuts = [128 * ((tiles * part) // 4) for part in range(5)]
    both = jnp.stack([block, owner_swap(block, "z")])
    chunks = [both[:, :, cuts[part] : cuts[part + 1]] for part in range(4)]
    for step in range(4):
        arrived = [owner_swap(chunk, order[step]) for chunk, order in zip(chunks, ORDERS)]
        chunks = [jnp.concatenate([chunk, new]) for chunk, new in zip(chunks, arrived)]
    return [chunk.reshape(-1, chunk.shape[-1]) for chunk in chunks], cuts


def scale_maps(in_maps, out_maps, col_scale, row_scale):
    scaled = [
        (maps[layer].astype(F32) * scale[layer][None, :]).astype(BF16)
        for maps, scale in ((out_maps, row_scale), (in_maps, col_scale))
        for layer in range(maps.shape[0])
    ]
    return jnp.concatenate(scaled, axis=1)


def common_order(chunk, order):
    parts = chunk.reshape(2, 2, 2, 2, 2, 8, chunk.shape[1])
    axes = [3 - order.index(name) for name in COMMON]
    return parts.transpose(axes + [4, 5, 6]).reshape(chunk.shape)


def one_hot(indices, size):
    return (indices[:, None] == jnp.arange(size, dtype=jnp.int32)[None, :]).astype(F32)


def turned_weights(white_left, white_right, owner, chip, core):
    rows = white_left.shape[1]
    line = jnp.arange(rows, dtype=jnp.int32)
    masks = jnp.asarray(held_masks(COMMON[::-1]), jnp.int32)
    contracted = one_hot((owner ^ jnp.repeat(masks, 8)) * 8 + line % 8, rows)
    away, there = core ^ (line // 128), (chip + line // 32) & 3
    exact = lax.Precision.HIGHEST
    left_rows = one_hot(128 * away + 32 * there + line % 32, rows)
    right_rows = one_hot(64 * there + 32 * away + line % 32, rows)
    left, right = [], []
    for layer in range(white_left.shape[0]):
        half = jnp.dot(left_rows, white_left[layer], precision=exact)
        left.append(lax.dot_general(half, contracted, NT, precision=exact))
        half = lax.dot_general(
            right_rows, white_right[layer], (((1,), (1,)), ((), ())), precision=exact
        )
        right.append(lax.dot_general(half, contracted, NT, precision=exact))
    return left, right


def absolute_chunks(parts, core, chip):
    two = jnp.roll(parts, 2, axis=2)
    parts = jnp.where(chip >= 2, two, parts)
    one = jnp.roll(parts, 1, axis=2)
    parts = jnp.where(chip % 2 == 1, one, parts)
    return jnp.where(core == 0, parts, parts[:, ::-1])


def tensor_sum(parts):
    jobs, rows, tokens = parts.shape[0], parts.shape[1] // 2, parts.shape[2]
    mine, theirs = parts[:, :rows], parts[:, rows:].astype(BF16)
    other = core_swap(theirs)
    both = (mine + other.astype(F32)).reshape(jobs, 4, rows // 4, tokens)
    sends = [chip_shift(both[:, step].astype(BF16), step) for step in (2, 1, 3)]
    total = both[:, 0] + sends[0].astype(F32) + sends[1].astype(F32) + sends[2].astype(F32)
    return total.astype(BF16)


def chip_swap(value, mask):
    pairs = [(src, src ^ (2 * mask)) for src in range(lax.axis_size("tensor"))]
    return lax.ppermute(value, "tensor", pairs)


def body(
    activations,
    out_grads,
    in_maps,
    out_maps,
    col_scale,
    row_scale,
    white_left,
    white_right,
    doc_lengths,
    queries,
):
    layers, tokens, hidden = activations.shape
    width = out_grads.shape[2]
    owners = lax.axis_size("fsdp")
    group = lax.axis_size("tensor")
    place = lax.axis_index("tensor")
    owner = lax.axis_index("fsdp")
    chip, core = place // 2, place % 2
    docs = doc_lengths.shape[1]
    own_queries, _, kout, kslice = queries.shape
    kin = kslice * group
    total_queries = own_queries * owners
    count = layers * kout * kin
    pair = layers * kslice // owners

    left_weights, right_weights = turned_weights(white_left, white_right, owner, chip, core)
    slices = queries.transpose(0, 1, 3, 2).reshape(own_queries, owners, pair * kout)
    slices = slices.transpose(1, 0, 2)
    chunks, cuts = tree_gather(scale_maps(in_maps, out_maps, col_scale, row_scale))

    chunks = [common_order(chunk, order) for chunk, order in zip(chunks, ORDERS)]
    parts = []
    for values, low, weights in (
        (out_grads, 0, left_weights),
        (activations, layers * width, right_weights),
    ):
        wide = values.shape[2]
        for layer in range(layers):
            first, total = low + layer * wide, None
            for index in range(4):
                begin, end = max(cuts[index], first), min(cuts[index + 1], first + wide)
                if begin >= end:
                    continue
                block = chunks[index][:, begin - cuts[index] : end - cuts[index]]
                piece = values[layer][:, begin - first : end - first]
                product = lax.dot_general(block, piece, NT, preferred_element_type=F32)
                total = product if total is None else total + product
            parts.append(jnp.dot(weights[layer], total, precision=lax.Precision.HIGH))
    summed = tensor_sum(jnp.stack(parts))
    left, right = summed[:layers], summed[layers:]
    around = [left] + [chip_shift(left, -step) for step in (1, 2, 3)]
    around = jnp.stack(around, axis=1)
    around = jnp.stack([around, core_swap(around)], axis=1)
    left_all = absolute_chunks(around, core, chip).reshape(layers, kout, tokens)

    lengths = doc_lengths[0]
    ends = jnp.cumsum(lengths)
    starts = ends - lengths
    spots = jnp.arange(tokens, dtype=jnp.int32)[None, :]
    member = ((spots >= starts[:, None]) & (spots < ends[:, None])).astype(BF16)
    features = []
    for layer in range(layers):
        masked = (right[layer][:, None, :] * member[None]).reshape(kslice * docs, tokens)
        features.append(
            lax.dot_general(masked, left_all[layer], NT, preferred_element_type=F32)
        )
    features = jnp.stack(features)
    doc_sq = jnp.sum((features * features).reshape(layers * kslice, docs, kout), axis=(0, 2))
    doc_sent = features.astype(BF16).reshape(owners, pair * docs, 2, kout // 2)
    doc_sent = doc_sent.transpose(0, 2, 1, 3).reshape(owners, 2 * pair * docs, kout // 2)
    sent = jnp.concatenate([slices, doc_sent], axis=2)
    got = lax.all_to_all(sent, "fsdp", 0, 0, tiled=True)
    query_got = got[:, :, : pair * kout].reshape(total_queries, pair * kout)
    query_f = query_got.astype(F32)
    query_sq = jnp.sum(query_f * query_f, axis=1)
    query_high = lax.reduce_precision(query_sq, 8, 7)
    query_low = query_sq - query_high

    doc_got = got[:, :, pair * kout :].reshape(owners, 2, pair * docs, kout // 2)
    doc_rows = doc_got.transpose(0, 2, 1, 3).reshape(owners * pair * docs, kout)
    half = (jnp.arange(owners * pair * docs) // docs) % pair
    wide = jnp.concatenate(
        [jnp.where((half == one)[:, None], doc_rows, 0) for one in range(pair)], axis=1
    )
    product = lax.dot_general(wide, query_got, NT, preferred_element_type=F32)
    product = product.reshape(owners, pair, docs, total_queries).sum(axis=1)
    extra = jnp.stack([query_high, query_low] + [jnp.zeros_like(query_low)] * 2)
    extra = jnp.broadcast_to(extra[None], (owners,) + extra.shape)
    score_sent = jnp.concatenate([product, extra], axis=1).astype(BF16)
    score_got = lax.all_to_all(score_sent, "fsdp", 0, 0, tiled=True)

    last = jnp.sum(score_got.astype(F32), axis=0)
    doc_row = jnp.pad(doc_sq, (0, total_queries - docs))[None]
    row = jnp.arange(2 * docs)[:, None]
    last = jnp.where(row == docs + 2, doc_row, last)
    last = last + core_swap(last)
    last = last + chip_swap(last, 1)
    last = last + chip_swap(last, 3)
    final = total_queries // group
    factor = 1.0 / math.sqrt(count)
    doc_scale = lax.rsqrt(last[docs + 2, :docs] / count + 1e-06) * factor
    mine = lax.dynamic_slice_in_dim(last[: docs + 2], place * final, final, axis=1)
    query_scale = lax.rsqrt((mine[docs] + mine[docs + 1]) / count + 1e-06)
    return mine[:docs] * doc_scale[:, None] * query_scale[None]


def solution(mesh):
    in_specs = (
        P(None, "fsdp", "tensor"),
        P(None, "fsdp", "tensor"),
        P(None, "fsdp", "tensor"),
        P(None, "fsdp", "tensor"),
        P(None, "tensor"),
        P(None, "tensor"),
        P(),
        P(),
        P("fsdp", None),
        P("fsdp", None, None, "tensor"),
    )
    out_specs = P("fsdp", "tensor")
    return jax.shard_map(body, mesh=mesh, in_specs=in_specs, out_specs=out_specs, check_vma=False)
```

time: 187 us -> 152 us (0.81)
  waiting for transfers between devices: 91.5 us -> 57.9 us
  starting transfers between devices: 47.6 us -> 60.7 us
  blocking collectives: 12 us -> 0 us
  local copies, waits for them, and re-layouts: 4.83 us -> 8.92 us
  other arithmetic: 10.5 us -> 6.91 us
  matrix products: 16.6 us -> 14.5 us
    all_to_all x1, waiting for transfers between devices: 75.4 us -> 11.3 us  [body(): got = lax.all_to_all(sent, 'fsdp', 0, 0, tiled=True)]
    ppermute x0 -> x19, starting transfers between devices: none -> 27.7 us  [the longest x17 22.6 us: owner_swap(): return lax.ppermute(value, 'fsdp', pairs)]
    ppermute x0 -> x19, waiting for transfers between devices: none -> 19.2 us  [the longest x17 13.8 us: owner_swap(): return lax.ppermute(value, 'fsdp', pairs)]
    ppermute x9 -> x6, waiting for transfers between devices: 4.16 us -> 16.5 us  [chip_shift(): lax.ppermute(value, 'tensor', [(src, (src + 2 * step) % size) for src in...]
    all_to_all x1 -> x0, blocking collectives: 12 us -> none  [body(): last = jnp.sum(lax.all_to_all(last, 'tensor', 0, 0, tiled=True), axis=0)]
    all_to_all x1 -> x0, starting transfers between devices: 7.89 us -> none  [body(): doc_got = lax.all_to_all(doc_sent, 'fsdp', 0, 0, tiled=True)]
    all_to_all x1 -> x0, waiting for transfers between devices: 5.21 us -> none  [body(): doc_got = lax.all_to_all(doc_sent, 'fsdp', 0, 0, tiled=True)]
    ppermute x9 -> x6, starting transfers between devices: 23.5 us -> 18.4 us  [chip_shift(): lax.ppermute(value, 'tensor', [(src, (src + 2 * step) % size) for src in...]
  transfers between devices with their start and end apart: 15 -> 30, of which waited for: 7 -> 19; matrix products, arithmetic and copies ran while one was open for 8% -> 11% of each run, Pallas kernels for 0% -> 0%
where the time goes in v2:
time: 152 us; the launch traced here: 150 us
  starting transfers between devices  60.7 us (40%)
  waiting for transfers between devices  57.9 us (38%)
  matrix products  14.5 us (10%)
  local copies, waits for them, and re-layouts  8.92 us (6%)
  other arithmetic  6.91 us (5%)
    ppermute x17, starting transfers between devices, owner_swap(): return lax.ppermute(value, 'fsdp', pairs)  22.6 us
    ppermute x6, starting transfers between devices, chip_shift(): lax.ppermute(value, 'tensor', [(src, (src + 2 * step) % size) for src in...  18.4 us
    ppermute x6, waiting for transfers between devices, chip_shift(): lax.ppermute(value, 'tensor', [(src, (src + 2 * step) % size) for src in...  16.5 us
    ppermute x17, waiting for transfers between devices, owner_swap(): return lax.ppermute(value, 'fsdp', pairs)  13.8 us
    all_to_all x1, waiting for transfers between devices, body(): got = lax.all_to_all(sent, 'fsdp', 0, 0, tiled=True)  11.3 us
    all_to_all x1, starting transfers between devices, body(): got = lax.all_to_all(sent, 'fsdp', 0, 0, tiled=True)  7.97 us
    all_to_all x1, waiting for transfers between devices, body(): score_got = lax.all_to_all(score_sent, 'fsdp', 0, 0, tiled=True)  6.68 us
    all_to_all x1, starting transfers between devices, body(): score_got = lax.all_to_all(score_sent, 'fsdp', 0, 0, tiled=True)  6.39 us
  transfers between devices with their start and end apart: 30, of which 19 were waited for; matrix products, arithmetic and copies ran while one was open for 11% of the time, Pallas kernels for 0%

profile of v2, /device:TPU:4, one launch (start us, length us, event | category | flops | bytes accessed | tf_op | source)
XLA Modules:
  0.0 149.8 jit_solution(4801764956575212681)
XLA Ops:
  3.3 2.0 %collective-permute-start = (bf16[8,8192]{1,0:T(8,128)(2,1)S(1)}, bf16[8,8192]{1,0:T(8,128)(2,1)S(1)}, u32[]{:S(2)}, u32[]{:S(2)}) collective-permute-start(bf16[8,8192]{1,0:T(8,128)(2,1)S(1)} %get-tuple-element.41), channel_id=1, source_target_pairs={{0,8},{8,0},{16,24},{24,16},{32,40},{40,32},{48,56},{56,48},{64,72... | collective-permute-start | bytes 393224 | tf_op jit(solution)/shard_map/ppermute | solution.py:42
  10.7 3.9 %slice_bitcast_fusion.1 = (bf16[640,3456]{1,0:T(8,128)(2,1)S(1)}, bf16[640,3456]{1,0:T(8,128)(2,1)S(1)}) fusion(bf16[2,640,3456]{2,1,0:T(8,128)(2,1)} %param.11), kind=kLoop, calls=%fused_computation.1 | loop fusion | bytes 17694720 | tf_op jit(solution)/shard_map/squeeze | solution.py:167
  15.9 3.1 %collective-permute-start.13 = (bf16[2,8,2048]{2,1,0:T(8,128)(2,1)S(1)}, bf16[2,8,2048]{2,1,0:T(8,128)(2,1)S(1)}, u32[]{:S(2)}, u32[]{:S(2)}) collective-permute-start(bf16[2,8,2048]{2,1,0:T(8,128)(2,1)S(1)} %get-tuple-element.31), channel_id=1, source_target_pairs={{0,48},{8,56},{16,32},{24,40},{32,16},{40,24},{48,0},{56,8},{64,11... | collective-permute-start | bytes 196616 | tf_op jit(solution)/shard_map/ppermute | solution.py:42
  21.5 1.4 collective-permute-start.14
  22.9 1.5 %collective-permute-done.9 = bf16[2,8,2048]{2,1,0:T(8,128)(2,1)S(1)} collective-permute-done((bf16[2,8,2048]{2,1,0:T(8,128)(2,1)S(1)}, bf16[2,8,2048]{2,1,0:T(8,128)(2,1)S(1)}, u32[]{:S(2)}, u32[]{:S(2)}) %collective-permute-start.9) | collective-permute-done | bytes 65568 | tf_op jit(solution)/shard_map/ppermute | solution.py:42
  25.4 2.1 %collective-permute-start.6 = (bf16[4,8,2048]{2,1,0:T(8,128)(2,1)S(1)}, bf16[4,8,2048]{2,1,0:T(8,128)(2,1)S(1)}, u32[]{:S(2)}, u32[]{:S(2)}) collective-permute-start(bf16[4,8,2048]{2,1,0:T(8,128)(2,1)S(1)} %pad_maximum_fusion.16), channel_id=1, source_target_pairs={{0,64},{8,72},{16,80},{24,88},{32,96},{40,104},{48,112},{56,120},{... | collective-permute-start | bytes 393224 | tf_op jit(solution)/shard_map/ppermute | solution.py:42
  27.6 1.4 collective-permute-start.15
  29.0 1.7 %collective-permute-done.10 = bf16[4,8,2048]{2,1,0:T(8,128)(2,1)S(1)} collective-permute-done((bf16[4,8,2048]{2,1,0:T(8,128)(2,1)S(1)}, bf16[4,8,2048]{2,1,0:T(8,128)(2,1)S(1)}, u32[]{:S(2)}, u32[]{:S(2)}) %collective-permute-start.10) | collective-permute-done | bytes 131104 | tf_op jit(solution)/shard_map/ppermute | solution.py:42
  30.7 1.4 collective-permute-start.11
  32.7 2.2 %collective-permute-start.7 = (bf16[8,8,2048]{2,1,0:T(8,128)(2,1)S(1)}, bf16[8,8,2048]{2,1,0:T(8,128)(2,1)S(1)}, u32[]{:S(2)}, u32[]{:S(2)}) collective-permute-start(bf16[8,8,2048]{2,1,0:T(8,128)(2,1)S(1)} %pad_maximum_fusion.9), channel_id=1, source_target_pairs={{0,48},{8,56},{16,32},{24,40},{32,16},{40,24},{48,0},{56,8},{64,11... | collective-permute-start | bytes 786440 | tf_op jit(solution)/shard_map/ppermute | solution.py:42
  35.1 2.2 %collective-permute-start.16 = (bf16[16,8,2048]{2,1,0:T(8,128)(2,1)S(1)}, bf16[16,8,2048]{2,1,0:T(8,128)(2,1)S(1)}, u32[]{:S(2)}, u32[]{:S(2)}) collective-permute-start(bf16[16,8,2048]{2,1,0:T(8,128)(2,1)S(1)} %pad_maximum_fusion.6), channel_id=1, source_target_pairs={{0,64},{8,72},{16,80},{24,88},{32,96},{40,104},{48,112},{56,120},{... | collective-permute-start | bytes 1572872 | tf_op jit(solution)/shard_map/ppermute | solution.py:42
  38.7 2.4 %collective-permute-start.4 = (bf16[16,8,2048]{2,1,0:T(8,128)(2,1)S(1)}, bf16[16,8,2048]{2,1,0:T(8,128)(2,1)S(1)}, u32[]{:S(2)}, u32[]{:S(2)}) collective-permute-start(bf16[16,8,2048]{2,1,0:T(8,128)(2,1)S(1)} %pad_maximum_fusion.3), channel_id=1, source_target_pairs={{0,48},{8,56},{16,32},{24,40},{32,16},{40,24},{48,0},{56,8},{64,11... | collective-permute-start | bytes 1572872 | tf_op jit(solution)/shard_map/ppermute | solution.py:42
  41.1 1.4 collective-permute-start.8
  42.7 5.8 %collective-permute-done.16 = bf16[16,8,2048]{2,1,0:T(8,128)(2,1)S(1)} collective-permute-done((bf16[16,8,2048]{2,1,0:T(8,128)(2,1)S(1)}, bf16[16,8,2048]{2,1,0:T(8,128)(2,1)S(1)}, u32[]{:S(2)}, u32[]{:S(2)}) %collective-permute-start.16) | collective-permute-done | bytes 524320 | tf_op jit(solution)/shard_map/ppermute | solution.py:42
  48.6 3.1 %collective-permute-done.4 = bf16[16,8,2048]{2,1,0:T(8,128)(2,1)S(1)} collective-permute-done((bf16[16,8,2048]{2,1,0:T(8,128)(2,1)S(1)}, bf16[16,8,2048]{2,1,0:T(8,128)(2,1)S(1)}, u32[]{:S(2)}, u32[]{:S(2)}) %collective-permute-start.4) | collective-permute-done | bytes 524320 | tf_op jit(solution)/shard_map/ppermute | solution.py:42
  59.8 1.8 %collective-permute-done.17 = bf16[4,128,640]{2,1,0:T(8,128)(2,1)} collective-permute-done((bf16[4,128,640]{2,1,0:T(8,128)(2,1)S(1)}, bf16[4,128,640]{2,1,0:T(8,128)(2,1)}, u32[]{:S(2)}, u32[]{:S(2)}) %collective-permute-start.17) | collective-permute-done | bytes 655392 | tf_op jit(solution)/shard_map/ppermute | solution.py:31
  62.9 5.6 %collective-permute-start.20 = (bf16[4,32,640]{2,1,0:T(8,128)(2,1)S(1)}, bf16[4,32,640]{2,1,0:T(8,128)(2,1)S(1)}, u32[]{:S(2)}, u32[]{:S(2)}) collective-permute-start(bf16[4,32,640]{2,1,0:T(8,128)(2,1)S(1)} %get-tuple-element.24), channel_id=1, source_target_pairs={{0,6},{1,7},{2,0},{3,1},{4,2},{5,3},{6,4},{7,5},{8,14},{9,15},{10,... | collective-permute-start | bytes 491528 | tf_op jit(solution)/shard_map/ppermute | solution.py:36
  68.4 3.8 %collective-permute-start.18 = (bf16[4,32,640]{2,1,0:T(8,128)(2,1)S(1)}, bf16[4,32,640]{2,1,0:T(8,128)(2,1)S(1)}, u32[]{:S(2)}, u32[]{:S(2)}) collective-permute-start(bf16[4,32,640]{2,1,0:T(8,128)(2,1)S(1)} %get-tuple-element.23), channel_id=1, source_target_pairs={{0,4},{1,5},{2,6},{3,7},{4,0},{5,1},{6,2},{7,3},{8,12},{9,13},{10,... | collective-permute-start | bytes 491528 | tf_op jit(solution)/shard_map/ppermute | solution.py:36
  72.2 2.0 %collective-permute-done.20 = bf16[4,32,640]{2,1,0:T(8,128)(2,1)S(1)} collective-permute-done((bf16[4,32,640]{2,1,0:T(8,128)(2,1)S(1)}, bf16[4,32,640]{2,1,0:T(8,128)(2,1)S(1)}, u32[]{:S(2)}, u32[]{:S(2)}) %collective-permute-start.20) | collective-permute-done | bytes 163872 | tf_op jit(solution)/shard_map/ppermute | solution.py:36
  74.2 8.9 %collective-permute-done.19 = bf16[4,32,640]{2,1,0:T(8,128)(2,1)S(1)} collective-permute-done((bf16[4,32,640]{2,1,0:T(8,128)(2,1)S(1)}, bf16[4,32,640]{2,1,0:T(8,128)(2,1)S(1)}, u32[]{:S(2)}, u32[]{:S(2)}) %collective-permute-start.19) | collective-permute-done | bytes 163872 | tf_op jit(solution)/shard_map/ppermute | solution.py:36
  83.7 5.4 %collective-permute-start.23 = (bf16[2,32,640]{2,1,0:T(8,128)(2,1)S(1)}, bf16[2,32,640]{2,1,0:T(8,128)(2,1)S(1)}, u32[]{:S(2)}, u32[]{:S(2)}) collective-permute-start(bf16[2,32,640]{2,1,0:T(8,128)(2,1)S(1)} %get-tuple-element.37), channel_id=1, source_target_pairs={{0,2},{1,3},{2,4},{3,5},{4,6},{5,7},{6,0},{7,1},{8,10},{9,11},{10,... | collective-permute-start | bytes 245768 | tf_op jit(solution)/shard_map/ppermute | solution.py:36
  89.0 2.0 %collective-permute-start.22 = (bf16[2,32,640]{2,1,0:T(8,128)(2,1)S(1)}, bf16[2,32,640]{2,1,0:T(8,128)(2,1)S(1)}, u32[]{:S(2)}, u32[]{:S(2)}) collective-permute-start(bf16[2,32,640]{2,1,0:T(8,128)(2,1)S(1)} %get-tuple-element.37), channel_id=1, source_target_pairs={{0,4},{1,5},{2,6},{3,7},{4,0},{5,1},{6,2},{7,3},{8,12},{9,13},{10,... | collective-permute-start | bytes 245768 | tf_op jit(solution)/shard_map/ppermute | solution.py:36
  91.0 1.7 %collective-permute-start.21 = (bf16[2,32,640]{2,1,0:T(8,128)(2,1)S(1)}, bf16[2,32,640]{2,1,0:T(8,128)(2,1)S(1)}, u32[]{:S(2)}, u32[]{:S(2)}) collective-permute-start(bf16[2,32,640]{2,1,0:T(8,128)(2,1)S(1)} %get-tuple-element.37), channel_id=1, source_target_pairs={{0,6},{1,7},{2,0},{3,1},{4,2},{5,3},{6,4},{7,5},{8,14},{9,15},{10,... | collective-permute-start | bytes 245768 | tf_op jit(solution)/shard_map/ppermute | solution.py:36
  93.3 5.0 %collective-permute-done.22 = bf16[2,32,640]{2,1,0:T(8,128)(2,1)S(1)} collective-permute-done((bf16[2,32,640]{2,1,0:T(8,128)(2,1)S(1)}, bf16[2,32,640]{2,1,0:T(8,128)(2,1)S(1)}, u32[]{:S(2)}, u32[]{:S(2)}) %collective-permute-start.22) | collective-permute-done | bytes 81952 | tf_op jit(solution)/shard_map/ppermute | solution.py:36
  102.3 8.0 %all-to-all-start = ((bf16[32,16,640]{2,1,0:T(8,128)(2,1)}), bf16[32,16,640]{2,1,0:T(8,128)(2,1)S(1)}, u32[]{:S(2)}, u32[]{:S(2)}) async-start(bf16[32,16,640]{2,1,0:T(8,128)(2,1)} %pad_maximum_fusion.2), calls=%async_computation | async-start | bytes 1310720 | tf_op jit(solution)/shard_map/all_to_all | solution.py:194
  110.4 11.3 %all-to-all-done = bf16[32,16,640]{2,1,0:T(8,128)(2,1)S(1)} async-done(((bf16[32,16,640]{2,1,0:T(8,128)(2,1)}), bf16[32,16,640]{2,1,0:T(8,128)(2,1)S(1)}, u32[]{:S(2)}, u32[]{:S(2)}) %all-to-all-start) | async-done | bytes 655392 | tf_op jit(solution)/shard_map/all_to_all | solution.py:194
  123.7 6.4 %all-to-all-start.1 = ((bf16[32,8,512]{2,1,0:T(8,128)(2,1)}), bf16[32,8,512]{2,1,0:T(8,128)(2,1)S(1)}, u32[]{:S(2)}, u32[]{:S(2)}) async-start(bf16[32,8,512]{2,1,0:T(8,128)(2,1)} %copy.46), calls=%async_computation.1 | async-start | bytes 524288 | tf_op jit(solution)/shard_map/all_to_all | solution.py:212
  130.4 6.7 %all-to-all-done.1 = bf16[32,8,512]{2,1,0:T(8,128)(2,1)S(1)} async-done(((bf16[32,8,512]{2,1,0:T(8,128)(2,1)}), bf16[32,8,512]{2,1,0:T(8,128)(2,1)S(1)}, u32[]{:S(2)}, u32[]{:S(2)}) %all-to-all-start.1) | async-done | bytes 262176 | tf_op jit(solution)/shard_map/all_to_all | solution.py:212
  138.5 2.8 %collective-permute-start.26 = (f32[8,512]{1,0:T(8,128)S(1)}, f32[8,512]{1,0:T(8,128)S(1)}, u32[]{:S(2)}, u32[]{:S(2)}) collective-permute-start(f32[8,512]{1,0:T(8,128)S(1)} %fusion.113), channel_id=1, source_target_pairs={{0,2},{1,3},{2,0},{3,1},{4,6},{5,7},{6,4},{7,5},{8,10},{9,11},{10,... | collective-permute-start | bytes 49160 | tf_op jit(solution)/shard_map/ppermute | solution.py:119
  141.2 1.9 %collective-permute-done.26 = f32[8,512]{1,0:T(8,128)S(1)} collective-permute-done((f32[8,512]{1,0:T(8,128)S(1)}, f32[8,512]{1,0:T(8,128)S(1)}, u32[]{:S(2)}, u32[]{:S(2)}) %collective-permute-start.26) | collective-permute-done | bytes 16416 | tf_op jit(solution)/shard_map/ppermute | solution.py:119
  143.2 2.4 %collective-permute-start.27 = (f32[8,512]{1,0:T(8,128)S(1)}, f32[8,512]{1,0:T(8,128)S(1)}, u32[]{:S(2)}, u32[]{:S(2)}) collective-permute-start(f32[8,512]{1,0:T(8,128)S(1)} %add.204), channel_id=1, source_target_pairs={{0,6},{1,7},{2,4},{3,5},{4,2},{5,3},{6,0},{7,1},{8,14},{9,15},{10,... | collective-permute-start | bytes 49160 | tf_op jit(solution)/shard_map/ppermute | solution.py:119
  145.5 3.5 %collective-permute-done.27 = f32[8,512]{1,0:T(8,128)S(1)} collective-permute-done((f32[8,512]{1,0:T(8,128)S(1)}, f32[8,512]{1,0:T(8,128)S(1)}, u32[]{:S(2)}, u32[]{:S(2)}) %collective-permute-start.27) | collective-permute-done | bytes 16416 | tf_op jit(solution)/shard_map/ppermute | solution.py:119
  (156 shorter events, 34.6 us)
Async XLA Ops:
  0.0 10.5 %copy-start.3 = (s32[32]{0:T(128)S(1)}, s32[32]{0:T(128)}, u32[]{:S(2)}) copy-start(s32[32]{0:T(128)} %constant.165.clone) | copy-start | bytes 388
  3.3 12.6 %collective-permute-start = (bf16[8,8192]{1,0:T(8,128)(2,1)S(1)}, bf16[8,8192]{1,0:T(8,128)(2,1)S(1)}, u32[]{:S(2)}, u32[]{:S(2)}) collective-permute-start(bf16[8,8192]{1,0:T(8,128)(2,1)S(1)} %get-tuple-element.41), channel_id=1, source_target_pairs={{0,8},{8,0},{16,24},{24,16},{32,40},{40,32},{48,56},{56,48},{64,72... | collective-permute-start | bytes 393224 | tf_op jit(solution)/shard_map/ppermute | solution.py:42
  15.9 5.6 %collective-permute-start.13 = (bf16[2,8,2048]{2,1,0:T(8,128)(2,1)S(1)}, bf16[2,8,2048]{2,1,0:T(8,128)(2,1)S(1)}, u32[]{:S(2)}, u32[]{:S(2)}) collective-permute-start(bf16[2,8,2048]{2,1,0:T(8,128)(2,1)S(1)} %get-tuple-element.31), channel_id=1, source_target_pairs={{0,48},{8,56},{16,32},{24,40},{32,16},{40,24},{48,0},{56,8},{64,11... | collective-permute-start | bytes 196616 | tf_op jit(solution)/shard_map/ppermute | solution.py:42
  19.5 5.0 %collective-permute-start.9 = (bf16[2,8,2048]{2,1,0:T(8,128)(2,1)S(1)}, bf16[2,8,2048]{2,1,0:T(8,128)(2,1)S(1)}, u32[]{:S(2)}, u32[]{:S(2)}) collective-permute-start(bf16[2,8,2048]{2,1,0:T(8,128)(2,1)S(1)} %get-tuple-element.33), channel_id=1, source_target_pairs={{0,16},{8,24},{16,0},{24,8},{32,48},{40,56},{48,32},{56,40},{64,80... | collective-permute-start | bytes 196616 | tf_op jit(solution)/shard_map/ppermute | solution.py:42
  19.7 5.1 %collective-permute-start.1 = (bf16[2,8,2048]{2,1,0:T(8,128)(2,1)S(1)}, bf16[2,8,2048]{2,1,0:T(8,128)(2,1)S(1)}, u32[]{:S(2)}, u32[]{:S(2)}) collective-permute-start(bf16[2,8,2048]{2,1,0:T(8,128)(2,1)S(1)} %get-tuple-element.29), channel_id=1, source_target_pairs={{0,64},{8,72},{16,80},{24,88},{32,96},{40,104},{48,112},{56,120},{... | collective-permute-start | bytes 196616 | tf_op jit(solution)/shard_map/ppermute | solution.py:42
  20.9 4.5 %collective-permute-start.5 = (bf16[2,8,2048]{2,1,0:T(8,128)(2,1)S(1)}, bf16[2,8,2048]{2,1,0:T(8,128)(2,1)S(1)}, u32[]{:S(2)}, u32[]{:S(2)}) collective-permute-start(bf16[2,8,2048]{2,1,0:T(8,128)(2,1)S(1)} %get-tuple-element.10), channel_id=1, source_target_pairs={{0,192},{8,200},{16,208},{24,216},{32,224},{40,232},{48,240},{56,2... | collective-permute-start | bytes 196616 | tf_op jit(solution)/shard_map/ppermute | solution.py:42
  21.5 6.0 %collective-permute-start.14 = (bf16[4,8,2048]{2,1,0:T(8,128)(2,1)S(1)}, bf16[4,8,2048]{2,1,0:T(8,128)(2,1)S(1)}, u32[]{:S(2)}, u32[]{:S(2)}) collective-permute-start(bf16[4,8,2048]{2,1,0:T(8,128)(2,1)S(1)} %pad_maximum_fusion.18), channel_id=1, source_target_pairs={{0,16},{8,24},{16,0},{24,8},{32,48},{40,56},{48,32},{56,40},{64,80... | collective-permute-start | bytes 393224 | tf_op jit(solution)/shard_map/ppermute | solution.py:42
  24.4 6.3 %collective-permute-start.10 = (bf16[4,8,2048]{2,1,0:T(8,128)(2,1)S(1)}, bf16[4,8,2048]{2,1,0:T(8,128)(2,1)S(1)}, u32[]{:S(2)}, u32[]{:S(2)}) collective-permute-start(bf16[4,8,2048]{2,1,0:T(8,128)(2,1)S(1)} %pad_maximum_fusion.17), channel_id=1, source_target_pairs={{0,48},{8,56},{16,32},{24,40},{32,16},{40,24},{48,0},{56,8},{64,11... | collective-permute-start | bytes 393224 | tf_op jit(solution)/shard_map/ppermute | solution.py:42
  24.8 7.4 %collective-permute-start.2 = (bf16[4,8,2048]{2,1,0:T(8,128)(2,1)S(1)}, bf16[4,8,2048]{2,1,0:T(8,128)(2,1)S(1)}, u32[]{:S(2)}, u32[]{:S(2)}) collective-permute-start(bf16[4,8,2048]{2,1,0:T(8,128)(2,1)S(1)} %pad_maximum_fusion.15), channel_id=1, source_target_pairs={{0,192},{8,200},{16,208},{24,216},{32,224},{40,232},{48,240},{56,2... | collective-permute-start | bytes 393224 | tf_op jit(solution)/shard_map/ppermute | solution.py:42
  25.4 7.3 %collective-permute-start.6 = (bf16[4,8,2048]{2,1,0:T(8,128)(2,1)S(1)}, bf16[4,8,2048]{2,1,0:T(8,128)(2,1)S(1)}, u32[]{:S(2)}, u32[]{:S(2)}) collective-permute-start(bf16[4,8,2048]{2,1,0:T(8,128)(2,1)S(1)} %pad_maximum_fusion.16), channel_id=1, source_target_pairs={{0,64},{8,72},{16,80},{24,88},{32,96},{40,104},{48,112},{56,120},{... | collective-permute-start | bytes 393224 | tf_op jit(solution)/shard_map/ppermute | solution.py:42
  27.6 7.4 %collective-permute-start.15 = (bf16[8,8,2048]{2,1,0:T(8,128)(2,1)S(1)}, bf16[8,8,2048]{2,1,0:T(8,128)(2,1)S(1)}, u32[]{:S(2)}, u32[]{:S(2)}) collective-permute-start(bf16[8,8,2048]{2,1,0:T(8,128)(2,1)S(1)} %pad_maximum_fusion.11), channel_id=1, source_target_pairs={{0,192},{8,200},{16,208},{24,216},{32,224},{40,232},{48,240},{56,2... | collective-permute-start | bytes 786440 | tf_op jit(solution)/shard_map/ppermute | solution.py:42
  30.7 7.5 %collective-permute-start.11 = (bf16[8,8,2048]{2,1,0:T(8,128)(2,1)S(1)}, bf16[8,8,2048]{2,1,0:T(8,128)(2,1)S(1)}, u32[]{:S(2)}, u32[]{:S(2)}) collective-permute-start(bf16[8,8,2048]{2,1,0:T(8,128)(2,1)S(1)} %pad_maximum_fusion.10), channel_id=1, source_target_pairs={{0,64},{8,72},{16,80},{24,88},{32,96},{40,104},{48,112},{56,120},{... | collective-permute-start | bytes 786440 | tf_op jit(solution)/shard_map/ppermute | solution.py:42
  32.2 6.5 %collective-permute-start.3 = (bf16[8,8,2048]{2,1,0:T(8,128)(2,1)S(1)}, bf16[8,8,2048]{2,1,0:T(8,128)(2,1)S(1)}, u32[]{:S(2)}, u32[]{:S(2)}) collective-permute-start(bf16[8,8,2048]{2,1,0:T(8,128)(2,1)S(1)} %pad_maximum_fusion.8), channel_id=1, source_target_pairs={{0,16},{8,24},{16,0},{24,8},{32,48},{40,56},{48,32},{56,40},{64,80... | collective-permute-start | bytes 786440 | tf_op jit(solution)/shard_map/ppermute | solution.py:42
  32.7 8.4 %collective-permute-start.7 = (bf16[8,8,2048]{2,1,0:T(8,128)(2,1)S(1)}, bf16[8,8,2048]{2,1,0:T(8,128)(2,1)S(1)}, u32[]{:S(2)}, u32[]{:S(2)}) collective-permute-start(bf16[8,8,2048]{2,1,0:T(8,128)(2,1)S(1)} %pad_maximum_fusion.9), channel_id=1, source_target_pairs={{0,48},{8,56},{16,32},{24,40},{32,16},{40,24},{48,0},{56,8},{64,11... | collective-permute-start | bytes 786440 | tf_op jit(solution)/shard_map/ppermute | solution.py:42
  35.1 13.3 %collective-permute-start.16 = (bf16[16,8,2048]{2,1,0:T(8,128)(2,1)S(1)}, bf16[16,8,2048]{2,1,0:T(8,128)(2,1)S(1)}, u32[]{:S(2)}, u32[]{:S(2)}) collective-permute-start(bf16[16,8,2048]{2,1,0:T(8,128)(2,1)S(1)} %pad_maximum_fusion.6), channel_id=1, source_target_pairs={{0,64},{8,72},{16,80},{24,88},{32,96},{40,104},{48,112},{56,120},{... | collective-permute-start | bytes 1572872 | tf_op jit(solution)/shard_map/ppermute | solution.py:42
  38.3 16.0 %collective-permute-start.12 = (bf16[16,8,2048]{2,1,0:T(8,128)(2,1)S(1)}, bf16[16,8,2048]{2,1,0:T(8,128)(2,1)S(1)}, u32[]{:S(2)}, u32[]{:S(2)}) collective-permute-start(bf16[16,8,2048]{2,1,0:T(8,128)(2,1)S(1)} %pad_maximum_fusion.5), channel_id=1, source_target_pairs={{0,192},{8,200},{16,208},{24,216},{32,224},{40,232},{48,240},{56,2... | collective-permute-start | bytes 1572872 | tf_op jit(solution)/shard_map/ppermute | solution.py:42
  38.7 12.9 %collective-permute-start.4 = (bf16[16,8,2048]{2,1,0:T(8,128)(2,1)S(1)}, bf16[16,8,2048]{2,1,0:T(8,128)(2,1)S(1)}, u32[]{:S(2)}, u32[]{:S(2)}) collective-permute-start(bf16[16,8,2048]{2,1,0:T(8,128)(2,1)S(1)} %pad_maximum_fusion.3), channel_id=1, source_target_pairs={{0,48},{8,56},{16,32},{24,40},{32,16},{40,24},{48,0},{56,8},{64,11... | collective-permute-start | bytes 1572872 | tf_op jit(solution)/shard_map/ppermute | solution.py:42
  41.1 14.5 %collective-permute-start.8 = (bf16[16,8,2048]{2,1,0:T(8,128)(2,1)S(1)}, bf16[16,8,2048]{2,1,0:T(8,128)(2,1)S(1)}, u32[]{:S(2)}, u32[]{:S(2)}) collective-permute-start(bf16[16,8,2048]{2,1,0:T(8,128)(2,1)S(1)} %pad_maximum_fusion.4), channel_id=1, source_target_pairs={{0,16},{8,24},{16,0},{24,8},{32,48},{40,56},{48,32},{56,40},{64,80... | collective-permute-start | bytes 1572872 | tf_op jit(solution)/shard_map/ppermute | solution.py:42
  59.2 2.3 %collective-permute-start.17 = (bf16[4,128,640]{2,1,0:T(8,128)(2,1)S(1)}, bf16[4,128,640]{2,1,0:T(8,128)(2,1)}, u32[]{:S(2)}, u32[]{:S(2)}) collective-permute-start(bf16[4,128,640]{2,1,0:T(8,128)(2,1)S(1)} %slice.382), channel_id=1, source_target_pairs={{0,1},{1,0},{2,3},{3,2},{4,5},{5,4},{6,7},{7,6},{8,9},{9,8},{10,11... | collective-permute-start | bytes 1966088 | tf_op jit(solution)/shard_map/ppermute | solution.py:31
  62.7 30.1 %copy-start.1 = (bf16[16,2,256,32]{2,3,1,0:T(8,128)(2,1)S(1)}, bf16[16,2,256,32]{2,3,1,0:T(8,128)(2,1)}, u32[]{:S(2)}) copy-start(bf16[16,2,256,32]{2,3,1,0:T(8,128)(2,1)} %param.20) | copy-start | bytes 1572868
  62.9 11.4 %collective-permute-start.20 = (bf16[4,32,640]{2,1,0:T(8,128)(2,1)S(1)}, bf16[4,32,640]{2,1,0:T(8,128)(2,1)S(1)}, u32[]{:S(2)}, u32[]{:S(2)}) collective-permute-start(bf16[4,32,640]{2,1,0:T(8,128)(2,1)S(1)} %get-tuple-element.24), channel_id=1, source_target_pairs={{0,6},{1,7},{2,0},{3,1},{4,2},{5,3},{6,4},{7,5},{8,14},{9,15},{10,... | collective-permute-start | bytes 491528 | tf_op jit(solution)/shard_map/ppermute | solution.py:36
  68.4 14.7 %collective-permute-start.19 = (bf16[4,32,640]{2,1,0:T(8,128)(2,1)S(1)}, bf16[4,32,640]{2,1,0:T(8,128)(2,1)S(1)}, u32[]{:S(2)}, u32[]{:S(2)}) collective-permute-start(bf16[4,32,640]{2,1,0:T(8,128)(2,1)S(1)} %get-tuple-element.25), channel_id=1, source_target_pairs={{0,2},{1,3},{2,4},{3,5},{4,6},{5,7},{6,0},{7,1},{8,10},{9,11},{10,... | collective-permute-start | bytes 491528 | tf_op jit(solution)/shard_map/ppermute | solution.py:36
  68.4 15.1 %collective-permute-start.18 = (bf16[4,32,640]{2,1,0:T(8,128)(2,1)S(1)}, bf16[4,32,640]{2,1,0:T(8,128)(2,1)S(1)}, u32[]{:S(2)}, u32[]{:S(2)}) collective-permute-start(bf16[4,32,640]{2,1,0:T(8,128)(2,1)S(1)} %get-tuple-element.23), channel_id=1, source_target_pairs={{0,4},{1,5},{2,6},{3,7},{4,0},{5,1},{6,2},{7,3},{8,12},{9,13},{10,... | collective-permute-start | bytes 491528 | tf_op jit(solution)/shard_map/ppermute | solution.py:36
  83.7 9.6 %collective-permute-start.23 = (bf16[2,32,640]{2,1,0:T(8,128)(2,1)S(1)}, bf16[2,32,640]{2,1,0:T(8,128)(2,1)S(1)}, u32[]{:S(2)}, u32[]{:S(2)}) collective-permute-start(bf16[2,32,640]{2,1,0:T(8,128)(2,1)S(1)} %get-tuple-element.37), channel_id=1, source_target_pairs={{0,2},{1,3},{2,4},{3,5},{4,6},{5,7},{6,0},{7,1},{8,10},{9,11},{10,... | collective-permute-start | bytes 245768 | tf_op jit(solution)/shard_map/ppermute | solution.py:36
  89.0 9.2 %collective-permute-start.22 = (bf16[2,32,640]{2,1,0:T(8,128)(2,1)S(1)}, bf16[2,32,640]{2,1,0:T(8,128)(2,1)S(1)}, u32[]{:S(2)}, u32[]{:S(2)}) collective-permute-start(bf16[2,32,640]{2,1,0:T(8,128)(2,1)S(1)} %get-tuple-element.37), channel_id=1, source_target_pairs={{0,4},{1,5},{2,6},{3,7},{4,0},{5,1},{6,2},{7,3},{8,12},{9,13},{10,... | collective-permute-start | bytes 245768 | tf_op jit(solution)/shard_map/ppermute | solution.py:36
  91.0 7.4 %collective-permute-start.21 = (bf16[2,32,640]{2,1,0:T(8,128)(2,1)S(1)}, bf16[2,32,640]{2,1,0:T(8,128)(2,1)S(1)}, u32[]{:S(2)}, u32[]{:S(2)}) collective-permute-start(bf16[2,32,640]{2,1,0:T(8,128)(2,1)S(1)} %get-tuple-element.37), channel_id=1, source_target_pairs={{0,6},{1,7},{2,0},{3,1},{4,2},{5,3},{6,4},{7,5},{8,14},{9,15},{10,... | collective-permute-start | bytes 245768 | tf_op jit(solution)/shard_map/ppermute | solution.py:36
  98.5 1.7 %collective-permute-start.24 = (bf16[2,4,32,640]{3,2,0,1:T(8,128)(2,1)S(1)}, bf16[2,4,32,640]{3,2,0,1:T(8,128)(2,1)S(1)}, u32[]{:S(2)}, u32[]{:S(2)}) collective-permute-start(bf16[2,4,32,640]{3,2,0,1:T(8,128)(2,1)S(1)} %get-tuple-element.27), channel_id=1, source_target_pairs={{0,1},{1,0},{2,3},{3,2},{4,5},{5,4},{6,7},{7,6},{8,9},{9,8},{10,11... | collective-permute-start | bytes 983048 | tf_op jit(solution)/shard_map/ppermute | solution.py:31
  102.3 19.4 %all-to-all-start = ((bf16[32,16,640]{2,1,0:T(8,128)(2,1)}), bf16[32,16,640]{2,1,0:T(8,128)(2,1)S(1)}, u32[]{:S(2)}, u32[]{:S(2)}) async-start(bf16[32,16,640]{2,1,0:T(8,128)(2,1)} %pad_maximum_fusion.2), calls=%async_computation | async-start | bytes 1310720 | tf_op jit(solution)/shard_map/all_to_all | solution.py:194
  123.7 13.3 %all-to-all-start.1 = ((bf16[32,8,512]{2,1,0:T(8,128)(2,1)}), bf16[32,8,512]{2,1,0:T(8,128)(2,1)S(1)}, u32[]{:S(2)}, u32[]{:S(2)}) async-start(bf16[32,8,512]{2,1,0:T(8,128)(2,1)} %copy.46), calls=%async_computation.1 | async-start | bytes 524288 | tf_op jit(solution)/shard_map/all_to_all | solution.py:212
  137.2 1.2 collective-permute-start.25
  138.5 4.7 %collective-permute-start.26 = (f32[8,512]{1,0:T(8,128)S(1)}, f32[8,512]{1,0:T(8,128)S(1)}, u32[]{:S(2)}, u32[]{:S(2)}) collective-permute-start(f32[8,512]{1,0:T(8,128)S(1)} %fusion.113), channel_id=1, source_target_pairs={{0,2},{1,3},{2,0},{3,1},{4,6},{5,7},{6,4},{7,5},{8,10},{9,11},{10,... | collective-permute-start | bytes 49160 | tf_op jit(solution)/shard_map/ppermute | solution.py:119
  143.2 5.8 %collective-permute-start.27 = (f32[8,512]{1,0:T(8,128)S(1)}, f32[8,512]{1,0:T(8,128)S(1)}, u32[]{:S(2)}, u32[]{:S(2)}) collective-permute-start(f32[8,512]{1,0:T(8,128)S(1)} %add.204), channel_id=1, source_target_pairs={{0,6},{1,7},{2,4},{3,5},{4,2},{5,3},{6,0},{7,1},{8,14},{9,15},{10,... | collective-permute-start | bytes 49160 | tf_op jit(solution)/shard_map/ppermute | solution.py:119
  (2 other events, 4.4 us)

commit v3 on v2

--- a/solution.py
+++ b/solution.py
@@ -46,15 +46,17 @@
     return lax.optimization_barrier((value,) + others)[0]
 
 
-def tree_gather(block):
+def tree_gather(block, rider):
     tiles = block.shape[1] // 128
     cuts = [128 * ((tiles * part) // 4) for part in range(5)]
     both = jnp.stack([block, owner_swap(block, "z")])
     chunks = [both[:, :, cuts[part] : cuts[part + 1]] for part in range(4)]
     for step in range(4):
+        if step == 3:
+            chunks[0], rider = lax.optimization_barrier((chunks[0], rider))
         arrived = [owner_swap(chunk, order[step]) for chunk, order in zip(chunks, ORDERS)]
         chunks = [jnp.concatenate([chunk, new]) for chunk, new in zip(chunks, arrived)]
-    return [chunk.reshape(-1, chunk.shape[-1]) for chunk in chunks], cuts
+    return [chunk.reshape(-1, chunk.shape[-1]) for chunk in chunks], cuts, rider
 
 
 def scale_maps(in_maps, out_maps, col_scale, row_scale):
@@ -82,7 +84,7 @@
     masks = jnp.asarray(held_masks(COMMON[::-1]), jnp.int32)
     contracted = one_hot((owner ^ jnp.repeat(masks, 8)) * 8 + line % 8, rows)
     away, there = core ^ (line // 128), (chip + line // 32) & 3
-    exact = lax.Precision.HIGHEST
+    exact = lax.Precision.HIGH
     left_rows = one_hot(128 * away + 32 * there + line % 32, rows)
     right_rows = one_hot(64 * there + 32 * away + line % 32, rows)
     left, right = [], []
@@ -145,10 +147,11 @@
     count = layers * kout * kin
     pair = layers * kslice // owners
 
-    left_weights, right_weights = turned_weights(white_left, white_right, owner, chip, core)
     slices = queries.transpose(0, 1, 3, 2).reshape(own_queries, owners, pair * kout)
     slices = slices.transpose(1, 0, 2)
-    chunks, cuts = tree_gather(scale_maps(in_maps, out_maps, col_scale, row_scale))
+    maps = scale_maps(in_maps, out_maps, col_scale, row_scale)
+    chunks, cuts, whites = tree_gather(maps, (white_left, white_right))
+    left_weights, right_weights = turned_weights(*whites, owner, chip, core)
 
     chunks = [common_order(chunk, order) for chunk, order in zip(chunks, ORDERS)]
     parts = []

time: 152 us -> 150 us (0.987)
  local copies, waits for them, and re-layouts: 8.92 us -> 13.3 us
  matrix products: 14.5 us -> 10.2 us
  waiting for transfers between devices: 57.9 us -> 55.2 us
    squeeze x1, local copies, waits for them, and re-layouts: 3.93 us -> 7.65 us  [body(): piece = values[layer][:, begin - first:end - first]]
    ppermute x17, waiting for transfers between devices: 13.8 us -> 10.6 us  [owner_swap(): return lax.ppermute(value, 'fsdp', pairs)]
    dot_general x2, matrix products: 2.59 us -> 0.56 us  [turned_weights(): lax.dot_general(right_rows, white_right[layer], (((1,), (1,)), ((), ())),...]
    dot_general x2, matrix products: 2.53 us -> 0.56 us  [turned_weights(): half = jnp.dot(left_rows, white_left[layer], precision=exact)]
  transfers between devices with their start and end apart: 30 -> 30, of which waited for: 19 -> 18; matrix products, arithmetic and copies ran while one was open for 11% -> 11% of each run, Pallas kernels for 0% -> 0%
where the time goes in v3:
time: 150 us; the launch traced here: 148 us
  starting transfers between devices  61.1 us (41%)
  waiting for transfers between devices  55.2 us (37%)
  local copies, waits for them, and re-layouts  13.3 us (9%)
  matrix products  10.2 us (7%)
  other arithmetic  7.62 us (5%)
    ppermute x17, starting transfers between devices, owner_swap(): return lax.ppermute(value, 'fsdp', pairs)  24 us
    ppermute x6, starting transfers between devices, chip_shift(): lax.ppermute(value, 'tensor', [(src, (src + 2 * step) % size) for src in...  18.3 us
    ppermute x6, waiting for transfers between devices, chip_shift(): lax.ppermute(value, 'tensor', [(src, (src + 2 * step) % size) for src in...  16.9 us
    all_to_all x1, waiting for transfers between devices, body(): got = lax.all_to_all(sent, 'fsdp', 0, 0, tiled=True)  11.3 us
    ppermute x17, waiting for transfers between devices, owner_swap(): return lax.ppermute(value, 'fsdp', pairs)  10.6 us
    squeeze x1, local copies, waits for them, and re-layouts, body(): piece = values[layer][:, begin - first:end - first]  7.65 us
    all_to_all x1, starting transfers between devices, body(): got = lax.all_to_all(sent, 'fsdp', 0, 0, tiled=True)  7.16 us
    all_to_all x1, waiting for transfers between devices, body(): score_got = lax.all_to_all(score_sent, 'fsdp', 0, 0, tiled=True)  6.68 us
  transfers between devices with their start and end apart: 30, of which 18 were waited for; matrix products, arithmetic and copies ran while one was open for 11% of the time, Pallas kernels for 0%

profile of v3, /device:TPU:4, one launch (start us, length us, event | category | flops | bytes accessed | tf_op | source)
XLA Modules:
  0.0 148.3 jit_solution(5630373785189740064)
XLA Ops:
  3.3 2.0 %collective-permute-start = (bf16[8,8192]{1,0:T(8,128)(2,1)S(1)}, bf16[8,8192]{1,0:T(8,128)(2,1)S(1)}, u32[]{:S(2)}, u32[]{:S(2)}) collective-permute-start(bf16[8,8192]{1,0:T(8,128)(2,1)S(1)} %get-tuple-element.43), channel_id=1, source_target_pairs={{0,8},{8,0},{16,24},{24,16},{32,40},{40,32},{48,56},{56,48},{64,72... | collective-permute-start | bytes 393224 | tf_op jit(solution)/shard_map/ppermute | solution.py:42
  6.1 7.7 %slice_bitcast_fusion.1 = (bf16[640,3456]{1,0:T(8,128)(2,1)}, bf16[640,3456]{1,0:T(8,128)(2,1)}) fusion(bf16[2,640,3456]{2,1,0:T(8,128)(2,1)} %param.11), kind=kLoop, calls=%fused_computation.1 | loop fusion | bytes 17694720 | tf_op jit(solution)/shard_map/squeeze | solution.py:170
  13.8 1.3 collective-permute-start.1
  15.1 3.0 %collective-permute-start.13 = (bf16[2,8,2048]{2,1,0:T(8,128)(2,1)S(1)}, bf16[2,8,2048]{2,1,0:T(8,128)(2,1)S(1)}, u32[]{:S(2)}, u32[]{:S(2)}) collective-permute-start(bf16[2,8,2048]{2,1,0:T(8,128)(2,1)S(1)} %get-tuple-element.34), channel_id=1, source_target_pairs={{0,48},{8,56},{16,32},{24,40},{32,16},{40,24},{48,0},{56,8},{64,11... | collective-permute-start | bytes 196616 | tf_op jit(solution)/shard_map/ppermute | solution.py:42
  18.3 2.1 %collective-permute-start.2 = (bf16[4,8,2048]{2,1,0:T(8,128)(2,1)S(1)}, bf16[4,8,2048]{2,1,0:T(8,128)(2,1)S(1)}, u32[]{:S(2)}, u32[]{:S(2)}) collective-permute-start(bf16[4,8,2048]{2,1,0:T(8,128)(2,1)S(1)} %pad_maximum_fusion.16), channel_id=1, source_target_pairs={{0,192},{8,200},{16,208},{24,216},{32,224},{40,232},{48,240},{56,2... | collective-permute-start | bytes 393224 | tf_op jit(solution)/shard_map/ppermute | solution.py:42
  20.6 1.8 %collective-permute-start.14 = (bf16[4,8,2048]{2,1,0:T(8,128)(2,1)S(1)}, bf16[4,8,2048]{2,1,0:T(8,128)(2,1)S(1)}, u32[]{:S(2)}, u32[]{:S(2)}) collective-permute-start(bf16[4,8,2048]{2,1,0:T(8,128)(2,1)S(1)} %pad_maximum_fusion.19), channel_id=1, source_target_pairs={{0,16},{8,24},{16,0},{24,8},{32,48},{40,56},{48,32},{56,40},{64,80... | collective-permute-start | bytes 393224 | tf_op jit(solution)/shard_map/ppermute | solution.py:42
  25.1 1.8 %collective-permute-start.3 = (bf16[8,8,2048]{2,1,0:T(8,128)(2,1)S(1)}, bf16[8,8,2048]{2,1,0:T(8,128)(2,1)S(1)}, u32[]{:S(2)}, u32[]{:S(2)}) collective-permute-start(bf16[8,8,2048]{2,1,0:T(8,128)(2,1)S(1)} %pad_maximum_fusion.9), channel_id=1, source_target_pairs={{0,16},{8,24},{16,0},{24,8},{32,48},{40,56},{48,32},{56,40},{64,80... | collective-permute-start | bytes 786440 | tf_op jit(solution)/shard_map/ppermute | solution.py:42
  29.4 1.5 %collective-permute-start.11 = (bf16[8,8,2048]{2,1,0:T(8,128)(2,1)S(1)}, bf16[8,8,2048]{2,1,0:T(8,128)(2,1)S(1)}, u32[]{:S(2)}, u32[]{:S(2)}) collective-permute-start(bf16[8,8,2048]{2,1,0:T(8,128)(2,1)S(1)} %pad_maximum_fusion.11), channel_id=1, source_target_pairs={{0,64},{8,72},{16,80},{24,88},{32,96},{40,104},{48,112},{56,120},{... | collective-permute-start | bytes 786440 | tf_op jit(solution)/shard_map/ppermute | solution.py:42
  31.0 2.0 %collective-permute-start.7 = (bf16[8,8,2048]{2,1,0:T(8,128)(2,1)S(1)}, bf16[8,8,2048]{2,1,0:T(8,128)(2,1)S(1)}, u32[]{:S(2)}, u32[]{:S(2)}) collective-permute-start(bf16[8,8,2048]{2,1,0:T(8,128)(2,1)S(1)} %pad_maximum_fusion.10), channel_id=1, source_target_pairs={{0,48},{8,56},{16,32},{24,40},{32,16},{40,24},{48,0},{56,8},{64,11... | collective-permute-start | bytes 786440 | tf_op jit(solution)/shard_map/ppermute | solution.py:42
  33.8 2.7 %collective-permute-start.16 = (bf16[16,8,2048]{2,1,0:T(8,128)(2,1)S(1)}, bf16[16,8,2048]{2,1,0:T(8,128)(2,1)S(1)}, u32[]{:S(2)}, u32[]{:S(2)}) collective-permute-start(bf16[16,8,2048]{2,1,0:T(8,128)(2,1)S(1)} %pad_maximum_fusion.7), channel_id=1, source_target_pairs={{0,64},{8,72},{16,80},{24,88},{32,96},{40,104},{48,112},{56,120},{... | collective-permute-start | bytes 1572872 | tf_op jit(solution)/shard_map/ppermute | solution.py:42
  37.0 1.3 collective-permute-done.11
  38.7 2.1 %collective-permute-start.4 = (bf16[16,8,2048]{2,1,0:T(8,128)(2,1)S(1)}, bf16[16,8,2048]{2,1,0:T(8,128)(2,1)S(1)}, u32[]{:S(2)}, u32[]{:S(2)}) collective-permute-start(bf16[16,8,2048]{2,1,0:T(8,128)(2,1)S(1)} %pad_maximum_fusion.4), channel_id=1, source_target_pairs={{0,48},{8,56},{16,32},{24,40},{32,16},{40,24},{48,0},{56,8},{64,11... | collective-permute-start | bytes 1572872 | tf_op jit(solution)/shard_map/ppermute | solution.py:42
  42.6 4.5 %collective-permute-done.16 = bf16[16,8,2048]{2,1,0:T(8,128)(2,1)S(1)} collective-permute-done((bf16[16,8,2048]{2,1,0:T(8,128)(2,1)S(1)}, bf16[16,8,2048]{2,1,0:T(8,128)(2,1)S(1)}, u32[]{:S(2)}, u32[]{:S(2)}) %collective-permute-start.16) | collective-permute-done | bytes 524320 | tf_op jit(solution)/shard_map/ppermute | solution.py:42
  47.3 2.6 %collective-permute-done.4 = bf16[16,8,2048]{2,1,0:T(8,128)(2,1)S(1)} collective-permute-done((bf16[16,8,2048]{2,1,0:T(8,128)(2,1)S(1)}, bf16[16,8,2048]{2,1,0:T(8,128)(2,1)S(1)}, u32[]{:S(2)}, u32[]{:S(2)}) %collective-permute-start.4) | collective-permute-done | bytes 524320 | tf_op jit(solution)/shard_map/ppermute | solution.py:42
  58.9 1.8 %collective-permute-done.17 = bf16[4,128,640]{2,1,0:T(8,128)(2,1)} collective-permute-done((bf16[4,128,640]{2,1,0:T(8,128)(2,1)S(1)}, bf16[4,128,640]{2,1,0:T(8,128)(2,1)}, u32[]{:S(2)}, u32[]{:S(2)}) %collective-permute-start.17) | collective-permute-done | bytes 655392 | tf_op jit(solution)/shard_map/ppermute | solution.py:31
  62.0 5.5 %collective-permute-start.20 = (bf16[4,32,640]{2,1,0:T(8,128)(2,1)S(1)}, bf16[4,32,640]{2,1,0:T(8,128)(2,1)S(1)}, u32[]{:S(2)}, u32[]{:S(2)}) collective-permute-start(bf16[4,32,640]{2,1,0:T(8,128)(2,1)S(1)} %get-tuple-element.28), channel_id=1, source_target_pairs={{0,6},{1,7},{2,0},{3,1},{4,2},{5,3},{6,4},{7,5},{8,14},{9,15},{10,... | collective-permute-start | bytes 491528 | tf_op jit(solution)/shard_map/ppermute | solution.py:36
  67.5 3.8 %collective-permute-start.18 = (bf16[4,32,640]{2,1,0:T(8,128)(2,1)S(1)}, bf16[4,32,640]{2,1,0:T(8,128)(2,1)S(1)}, u32[]{:S(2)}, u32[]{:S(2)}) collective-permute-start(bf16[4,32,640]{2,1,0:T(8,128)(2,1)S(1)} %get-tuple-element.27), channel_id=1, source_target_pairs={{0,4},{1,5},{2,6},{3,7},{4,0},{5,1},{6,2},{7,3},{8,12},{9,13},{10,... | collective-permute-start | bytes 491528 | tf_op jit(solution)/shard_map/ppermute | solution.py:36
  71.3 1.7 %collective-permute-done.20 = bf16[4,32,640]{2,1,0:T(8,128)(2,1)S(1)} collective-permute-done((bf16[4,32,640]{2,1,0:T(8,128)(2,1)S(1)}, bf16[4,32,640]{2,1,0:T(8,128)(2,1)S(1)}, u32[]{:S(2)}, u32[]{:S(2)}) %collective-permute-start.20) | collective-permute-done | bytes 163872 | tf_op jit(solution)/shard_map/ppermute | solution.py:36
  73.0 9.4 %collective-permute-done.19 = bf16[4,32,640]{2,1,0:T(8,128)(2,1)S(1)} collective-permute-done((bf16[4,32,640]{2,1,0:T(8,128)(2,1)S(1)}, bf16[4,32,640]{2,1,0:T(8,128)(2,1)S(1)}, u32[]{:S(2)}, u32[]{:S(2)}) %collective-permute-start.19) | collective-permute-done | bytes 163872 | tf_op jit(solution)/shard_map/ppermute | solution.py:36
  82.8 5.4 %collective-permute-start.23 = (bf16[2,32,640]{2,1,0:T(8,128)(2,1)S(1)}, bf16[2,32,640]{2,1,0:T(8,128)(2,1)S(1)}, u32[]{:S(2)}, u32[]{:S(2)}) collective-permute-start(bf16[2,32,640]{2,1,0:T(8,128)(2,1)S(1)} %get-tuple-element.40), channel_id=1, source_target_pairs={{0,2},{1,3},{2,4},{3,5},{4,6},{5,7},{6,0},{7,1},{8,10},{9,11},{10,... | collective-permute-start | bytes 245768 | tf_op jit(solution)/shard_map/ppermute | solution.py:36
  88.1 2.0 %collective-permute-start.22 = (bf16[2,32,640]{2,1,0:T(8,128)(2,1)S(1)}, bf16[2,32,640]{2,1,0:T(8,128)(2,1)S(1)}, u32[]{:S(2)}, u32[]{:S(2)}) collective-permute-start(bf16[2,32,640]{2,1,0:T(8,128)(2,1)S(1)} %get-tuple-element.40), channel_id=1, source_target_pairs={{0,4},{1,5},{2,6},{3,7},{4,0},{5,1},{6,2},{7,3},{8,12},{9,13},{10,... | collective-permute-start | bytes 245768 | tf_op jit(solution)/shard_map/ppermute | solution.py:36
  90.1 1.7 %collective-permute-start.21 = (bf16[2,32,640]{2,1,0:T(8,128)(2,1)S(1)}, bf16[2,32,640]{2,1,0:T(8,128)(2,1)S(1)}, u32[]{:S(2)}, u32[]{:S(2)}) collective-permute-start(bf16[2,32,640]{2,1,0:T(8,128)(2,1)S(1)} %get-tuple-element.40), channel_id=1, source_target_pairs={{0,6},{1,7},{2,0},{3,1},{4,2},{5,3},{6,4},{7,5},{8,14},{9,15},{10,... | collective-permute-start | bytes 245768 | tf_op jit(solution)/shard_map/ppermute | solution.py:36
  92.4 5.1 %collective-permute-done.22 = bf16[2,32,640]{2,1,0:T(8,128)(2,1)S(1)} collective-permute-done((bf16[2,32,640]{2,1,0:T(8,128)(2,1)S(1)}, bf16[2,32,640]{2,1,0:T(8,128)(2,1)S(1)}, u32[]{:S(2)}, u32[]{:S(2)}) %collective-permute-start.22) | collective-permute-done | bytes 81952 | tf_op jit(solution)/shard_map/ppermute | solution.py:36
  98.4 1.3 collective-permute-done.24
  101.7 7.2 %all-to-all-start = ((bf16[32,16,640]{2,1,0:T(8,128)(2,1)}), bf16[32,16,640]{2,1,0:T(8,128)(2,1)S(1)}, u32[]{:S(2)}, u32[]{:S(2)}) async-start(bf16[32,16,640]{2,1,0:T(8,128)(2,1)} %pad_maximum_fusion.3), calls=%async_computation | async-start | bytes 1310720 | tf_op jit(solution)/shard_map/all_to_all | solution.py:197
  109.0 11.3 %all-to-all-done = bf16[32,16,640]{2,1,0:T(8,128)(2,1)S(1)} async-done(((bf16[32,16,640]{2,1,0:T(8,128)(2,1)}), bf16[32,16,640]{2,1,0:T(8,128)(2,1)S(1)}, u32[]{:S(2)}, u32[]{:S(2)}) %all-to-all-start) | async-done | bytes 655392 | tf_op jit(solution)/shard_map/all_to_all | solution.py:197
  122.3 6.4 %all-to-all-start.1 = ((bf16[32,8,512]{2,1,0:T(8,128)(2,1)}), bf16[32,8,512]{2,1,0:T(8,128)(2,1)S(1)}, u32[]{:S(2)}, u32[]{:S(2)}) async-start(bf16[32,8,512]{2,1,0:T(8,128)(2,1)} %copy.46), calls=%async_computation.1 | async-start | bytes 524288 | tf_op jit(solution)/shard_map/all_to_all | solution.py:215
  129.0 6.7 %all-to-all-done.1 = bf16[32,8,512]{2,1,0:T(8,128)(2,1)S(1)} async-done(((bf16[32,8,512]{2,1,0:T(8,128)(2,1)}), bf16[32,8,512]{2,1,0:T(8,128)(2,1)S(1)}, u32[]{:S(2)}, u32[]{:S(2)}) %all-to-all-start.1) | async-done | bytes 262176 | tf_op jit(solution)/shard_map/all_to_all | solution.py:215
  137.1 2.7 %collective-permute-start.26 = (f32[8,512]{1,0:T(8,128)S(1)}, f32[8,512]{1,0:T(8,128)S(1)}, u32[]{:S(2)}, u32[]{:S(2)}) collective-permute-start(f32[8,512]{1,0:T(8,128)S(1)} %fusion.112), channel_id=1, source_target_pairs={{0,2},{1,3},{2,0},{3,1},{4,6},{5,7},{6,4},{7,5},{8,10},{9,11},{10,... | collective-permute-start | bytes 49160 | tf_op jit(solution)/shard_map/ppermute | solution.py:121
  139.7 2.0 %collective-permute-done.26 = f32[8,512]{1,0:T(8,128)S(1)} collective-permute-done((f32[8,512]{1,0:T(8,128)S(1)}, f32[8,512]{1,0:T(8,128)S(1)}, u32[]{:S(2)}, u32[]{:S(2)}) %collective-permute-start.26) | collective-permute-done | bytes 16416 | tf_op jit(solution)/shard_map/ppermute | solution.py:121
  141.7 2.3 %collective-permute-start.27 = (f32[8,512]{1,0:T(8,128)S(1)}, f32[8,512]{1,0:T(8,128)S(1)}, u32[]{:S(2)}, u32[]{:S(2)}) collective-permute-start(f32[8,512]{1,0:T(8,128)S(1)} %add.204), channel_id=1, source_target_pairs={{0,6},{1,7},{2,4},{3,5},{4,2},{5,3},{6,0},{7,1},{8,14},{9,15},{10,... | collective-permute-start | bytes 49160 | tf_op jit(solution)/shard_map/ppermute | solution.py:121
  144.0 3.5 %collective-permute-done.27 = f32[8,512]{1,0:T(8,128)S(1)} collective-permute-done((f32[8,512]{1,0:T(8,128)S(1)}, f32[8,512]{1,0:T(8,128)S(1)}, u32[]{:S(2)}, u32[]{:S(2)}) %collective-permute-start.27) | collective-permute-done | bytes 16416 | tf_op jit(solution)/shard_map/ppermute | solution.py:121
  (165 shorter events, 31.4 us)
Async XLA Ops:
  3.3 10.5 %collective-permute-start = (bf16[8,8192]{1,0:T(8,128)(2,1)S(1)}, bf16[8,8192]{1,0:T(8,128)(2,1)S(1)}, u32[]{:S(2)}, u32[]{:S(2)}) collective-permute-start(bf16[8,8192]{1,0:T(8,128)(2,1)S(1)} %get-tuple-element.43), channel_id=1, source_target_pairs={{0,8},{8,0},{16,24},{24,16},{32,40},{40,32},{48,56},{56,48},{64,72... | collective-permute-start | bytes 393224 | tf_op jit(solution)/shard_map/ppermute | solution.py:42
  13.8 4.5 %collective-permute-start.1 = (bf16[2,8,2048]{2,1,0:T(8,128)(2,1)S(1)}, bf16[2,8,2048]{2,1,0:T(8,128)(2,1)S(1)}, u32[]{:S(2)}, u32[]{:S(2)}) collective-permute-start(bf16[2,8,2048]{2,1,0:T(8,128)(2,1)S(1)} %get-tuple-element.32), channel_id=1, source_target_pairs={{0,64},{8,72},{16,80},{24,88},{32,96},{40,104},{48,112},{56,120},{... | collective-permute-start | bytes 196616 | tf_op jit(solution)/shard_map/ppermute | solution.py:42
  15.1 5.5 %collective-permute-start.13 = (bf16[2,8,2048]{2,1,0:T(8,128)(2,1)S(1)}, bf16[2,8,2048]{2,1,0:T(8,128)(2,1)S(1)}, u32[]{:S(2)}, u32[]{:S(2)}) collective-permute-start(bf16[2,8,2048]{2,1,0:T(8,128)(2,1)S(1)} %get-tuple-element.34), channel_id=1, source_target_pairs={{0,48},{8,56},{16,32},{24,40},{32,16},{40,24},{48,0},{56,8},{64,11... | collective-permute-start | bytes 196616 | tf_op jit(solution)/shard_map/ppermute | solution.py:42
  18.1 5.0 %collective-permute-start.9 = (bf16[2,8,2048]{2,1,0:T(8,128)(2,1)S(1)}, bf16[2,8,2048]{2,1,0:T(8,128)(2,1)S(1)}, u32[]{:S(2)}, u32[]{:S(2)}) collective-permute-start(bf16[2,8,2048]{2,1,0:T(8,128)(2,1)S(1)} %get-tuple-element.36), channel_id=1, source_target_pairs={{0,16},{8,24},{16,0},{24,8},{32,48},{40,56},{48,32},{56,40},{64,80... | collective-permute-start | bytes 196616 | tf_op jit(solution)/shard_map/ppermute | solution.py:42
  18.3 5.6 %collective-permute-start.5 = (bf16[2,8,2048]{2,1,0:T(8,128)(2,1)S(1)}, bf16[2,8,2048]{2,1,0:T(8,128)(2,1)S(1)}, u32[]{:S(2)}, u32[]{:S(2)}) collective-permute-start(bf16[2,8,2048]{2,1,0:T(8,128)(2,1)S(1)} %get-tuple-element.16), channel_id=1, source_target_pairs={{0,192},{8,200},{16,208},{24,216},{32,224},{40,232},{48,240},{56,2... | collective-permute-start | bytes 196616 | tf_op jit(solution)/shard_map/ppermute | solution.py:42
  18.3 6.7 %collective-permute-start.2 = (bf16[4,8,2048]{2,1,0:T(8,128)(2,1)S(1)}, bf16[4,8,2048]{2,1,0:T(8,128)(2,1)S(1)}, u32[]{:S(2)}, u32[]{:S(2)}) collective-permute-start(bf16[4,8,2048]{2,1,0:T(8,128)(2,1)S(1)} %pad_maximum_fusion.16), channel_id=1, source_target_pairs={{0,192},{8,200},{16,208},{24,216},{32,224},{40,232},{48,240},{56,2... | collective-permute-start | bytes 393224 | tf_op jit(solution)/shard_map/ppermute | solution.py:42
  20.6 6.3 %collective-permute-start.14 = (bf16[4,8,2048]{2,1,0:T(8,128)(2,1)S(1)}, bf16[4,8,2048]{2,1,0:T(8,128)(2,1)S(1)}, u32[]{:S(2)}, u32[]{:S(2)}) collective-permute-start(bf16[4,8,2048]{2,1,0:T(8,128)(2,1)S(1)} %pad_maximum_fusion.19), channel_id=1, source_target_pairs={{0,16},{8,24},{16,0},{24,8},{32,48},{40,56},{48,32},{56,40},{64,80... | collective-permute-start | bytes 393224 | tf_op jit(solution)/shard_map/ppermute | solution.py:42
  23.1 6.3 %collective-permute-start.10 = (bf16[4,8,2048]{2,1,0:T(8,128)(2,1)S(1)}, bf16[4,8,2048]{2,1,0:T(8,128)(2,1)S(1)}, u32[]{:S(2)}, u32[]{:S(2)}) collective-permute-start(bf16[4,8,2048]{2,1,0:T(8,128)(2,1)S(1)} %pad_maximum_fusion.18), channel_id=1, source_target_pairs={{0,48},{8,56},{16,32},{24,40},{32,16},{40,24},{48,0},{56,8},{64,11... | collective-permute-start | bytes 393224 | tf_op jit(solution)/shard_map/ppermute | solution.py:42
  23.9 7.0 %collective-permute-start.6 = (bf16[4,8,2048]{2,1,0:T(8,128)(2,1)S(1)}, bf16[4,8,2048]{2,1,0:T(8,128)(2,1)S(1)}, u32[]{:S(2)}, u32[]{:S(2)}) collective-permute-start(bf16[4,8,2048]{2,1,0:T(8,128)(2,1)S(1)} %pad_maximum_fusion.17), channel_id=1, source_target_pairs={{0,64},{8,72},{16,80},{24,88},{32,96},{40,104},{48,112},{56,120},{... | collective-permute-start | bytes 393224 | tf_op jit(solution)/shard_map/ppermute | solution.py:42
  25.1 8.0 %collective-permute-start.3 = (bf16[8,8,2048]{2,1,0:T(8,128)(2,1)S(1)}, bf16[8,8,2048]{2,1,0:T(8,128)(2,1)S(1)}, u32[]{:S(2)}, u32[]{:S(2)}) collective-permute-start(bf16[8,8,2048]{2,1,0:T(8,128)(2,1)S(1)} %pad_maximum_fusion.9), channel_id=1, source_target_pairs={{0,16},{8,24},{16,0},{24,8},{32,48},{40,56},{48,32},{56,40},{64,80... | collective-permute-start | bytes 786440 | tf_op jit(solution)/shard_map/ppermute | solution.py:42
  26.9 6.7 %collective-permute-start.15 = (bf16[8,8,2048]{2,1,0:T(8,128)(2,1)S(1)}, bf16[8,8,2048]{2,1,0:T(8,128)(2,1)S(1)}, u32[]{:S(2)}, u32[]{:S(2)}) collective-permute-start(bf16[8,8,2048]{2,1,0:T(8,128)(2,1)S(1)} %pad_maximum_fusion.12), channel_id=1, source_target_pairs={{0,192},{8,200},{16,208},{24,216},{32,224},{40,232},{48,240},{56,2... | collective-permute-start | bytes 786440 | tf_op jit(solution)/shard_map/ppermute | solution.py:42
  29.4 8.9 %collective-permute-start.11 = (bf16[8,8,2048]{2,1,0:T(8,128)(2,1)S(1)}, bf16[8,8,2048]{2,1,0:T(8,128)(2,1)S(1)}, u32[]{:S(2)}, u32[]{:S(2)}) collective-permute-start(bf16[8,8,2048]{2,1,0:T(8,128)(2,1)S(1)} %pad_maximum_fusion.11), channel_id=1, source_target_pairs={{0,64},{8,72},{16,80},{24,88},{32,96},{40,104},{48,112},{56,120},{... | collective-permute-start | bytes 786440 | tf_op jit(solution)/shard_map/ppermute | solution.py:42
  31.0 10.5 %collective-permute-start.7 = (bf16[8,8,2048]{2,1,0:T(8,128)(2,1)S(1)}, bf16[8,8,2048]{2,1,0:T(8,128)(2,1)S(1)}, u32[]{:S(2)}, u32[]{:S(2)}) collective-permute-start(bf16[8,8,2048]{2,1,0:T(8,128)(2,1)S(1)} %pad_maximum_fusion.10), channel_id=1, source_target_pairs={{0,48},{8,56},{16,32},{24,40},{32,16},{40,24},{48,0},{56,8},{64,11... | collective-permute-start | bytes 786440 | tf_op jit(solution)/shard_map/ppermute | solution.py:42
  33.7 16.4 %slice-start = ((s8[4423680]{0:T(1024)(128)(4,1)}), s8[4194304]{0:T(1024)(128)(4,1)S(1)}, s32[]{:S(2)}) async-start(s8[4423680]{0:T(1024)(128)(4,1)} %bitcast.153), calls=%async_computation.2 | async-start | bytes 8388608
  33.8 13.4 %collective-permute-start.16 = (bf16[16,8,2048]{2,1,0:T(8,128)(2,1)S(1)}, bf16[16,8,2048]{2,1,0:T(8,128)(2,1)S(1)}, u32[]{:S(2)}, u32[]{:S(2)}) collective-permute-start(bf16[16,8,2048]{2,1,0:T(8,128)(2,1)S(1)} %pad_maximum_fusion.7), channel_id=1, source_target_pairs={{0,64},{8,72},{16,80},{24,88},{32,96},{40,104},{48,112},{56,120},{... | collective-permute-start | bytes 1572872 | tf_op jit(solution)/shard_map/ppermute | solution.py:42
  38.4 15.0 %collective-permute-start.12 = (bf16[16,8,2048]{2,1,0:T(8,128)(2,1)S(1)}, bf16[16,8,2048]{2,1,0:T(8,128)(2,1)S(1)}, u32[]{:S(2)}, u32[]{:S(2)}) collective-permute-start(bf16[16,8,2048]{2,1,0:T(8,128)(2,1)S(1)} %pad_maximum_fusion.6), channel_id=1, source_target_pairs={{0,192},{8,200},{16,208},{24,216},{32,224},{40,232},{48,240},{56,2... | collective-permute-start | bytes 1572872 | tf_op jit(solution)/shard_map/ppermute | solution.py:42
  38.7 11.2 %collective-permute-start.4 = (bf16[16,8,2048]{2,1,0:T(8,128)(2,1)S(1)}, bf16[16,8,2048]{2,1,0:T(8,128)(2,1)S(1)}, u32[]{:S(2)}, u32[]{:S(2)}) collective-permute-start(bf16[16,8,2048]{2,1,0:T(8,128)(2,1)S(1)} %pad_maximum_fusion.4), channel_id=1, source_target_pairs={{0,48},{8,56},{16,32},{24,40},{32,16},{40,24},{48,0},{56,8},{64,11... | collective-permute-start | bytes 1572872 | tf_op jit(solution)/shard_map/ppermute | solution.py:42
  41.5 13.2 %collective-permute-start.8 = (bf16[16,8,2048]{2,1,0:T(8,128)(2,1)S(1)}, bf16[16,8,2048]{2,1,0:T(8,128)(2,1)S(1)}, u32[]{:S(2)}, u32[]{:S(2)}) collective-permute-start(bf16[16,8,2048]{2,1,0:T(8,128)(2,1)S(1)} %pad_maximum_fusion.5), channel_id=1, source_target_pairs={{0,16},{8,24},{16,0},{24,8},{32,48},{40,56},{48,32},{56,40},{64,80... | collective-permute-start | bytes 1572872 | tf_op jit(solution)/shard_map/ppermute | solution.py:42
  58.3 2.3 %collective-permute-start.17 = (bf16[4,128,640]{2,1,0:T(8,128)(2,1)S(1)}, bf16[4,128,640]{2,1,0:T(8,128)(2,1)}, u32[]{:S(2)}, u32[]{:S(2)}) collective-permute-start(bf16[4,128,640]{2,1,0:T(8,128)(2,1)S(1)} %slice.382), channel_id=1, source_target_pairs={{0,1},{1,0},{2,3},{3,2},{4,5},{5,4},{6,7},{7,6},{8,9},{9,8},{10,11... | collective-permute-start | bytes 1966088 | tf_op jit(solution)/shard_map/ppermute | solution.py:31
  61.9 30.0 %copy-start.3 = (bf16[16,2,256,32]{2,3,1,0:T(8,128)(2,1)S(1)}, bf16[16,2,256,32]{2,3,1,0:T(8,128)(2,1)}, u32[]{:S(2)}) copy-start(bf16[16,2,256,32]{2,3,1,0:T(8,128)(2,1)} %param.20) | copy-start | bytes 1572868
  62.0 11.0 %collective-permute-start.20 = (bf16[4,32,640]{2,1,0:T(8,128)(2,1)S(1)}, bf16[4,32,640]{2,1,0:T(8,128)(2,1)S(1)}, u32[]{:S(2)}, u32[]{:S(2)}) collective-permute-start(bf16[4,32,640]{2,1,0:T(8,128)(2,1)S(1)} %get-tuple-element.28), channel_id=1, source_target_pairs={{0,6},{1,7},{2,0},{3,1},{4,2},{5,3},{6,4},{7,5},{8,14},{9,15},{10,... | collective-permute-start | bytes 491528 | tf_op jit(solution)/shard_map/ppermute | solution.py:36
  67.5 15.0 %collective-permute-start.19 = (bf16[4,32,640]{2,1,0:T(8,128)(2,1)S(1)}, bf16[4,32,640]{2,1,0:T(8,128)(2,1)S(1)}, u32[]{:S(2)}, u32[]{:S(2)}) collective-permute-start(bf16[4,32,640]{2,1,0:T(8,128)(2,1)S(1)} %get-tuple-element.29), channel_id=1, source_target_pairs={{0,2},{1,3},{2,4},{3,5},{4,6},{5,7},{6,0},{7,1},{8,10},{9,11},{10,... | collective-permute-start | bytes 491528 | tf_op jit(solution)/shard_map/ppermute | solution.py:36
  67.5 15.2 %collective-permute-start.18 = (bf16[4,32,640]{2,1,0:T(8,128)(2,1)S(1)}, bf16[4,32,640]{2,1,0:T(8,128)(2,1)S(1)}, u32[]{:S(2)}, u32[]{:S(2)}) collective-permute-start(bf16[4,32,640]{2,1,0:T(8,128)(2,1)S(1)} %get-tuple-element.27), channel_id=1, source_target_pairs={{0,4},{1,5},{2,6},{3,7},{4,0},{5,1},{6,2},{7,3},{8,12},{9,13},{10,... | collective-permute-start | bytes 491528 | tf_op jit(solution)/shard_map/ppermute | solution.py:36
  82.8 9.6 %collective-permute-start.23 = (bf16[2,32,640]{2,1,0:T(8,128)(2,1)S(1)}, bf16[2,32,640]{2,1,0:T(8,128)(2,1)S(1)}, u32[]{:S(2)}, u32[]{:S(2)}) collective-permute-start(bf16[2,32,640]{2,1,0:T(8,128)(2,1)S(1)} %get-tuple-element.40), channel_id=1, source_target_pairs={{0,2},{1,3},{2,4},{3,5},{4,6},{5,7},{6,0},{7,1},{8,10},{9,11},{10,... | collective-permute-start | bytes 245768 | tf_op jit(solution)/shard_map/ppermute | solution.py:36
  88.1 9.4 %collective-permute-start.22 = (bf16[2,32,640]{2,1,0:T(8,128)(2,1)S(1)}, bf16[2,32,640]{2,1,0:T(8,128)(2,1)S(1)}, u32[]{:S(2)}, u32[]{:S(2)}) collective-permute-start(bf16[2,32,640]{2,1,0:T(8,128)(2,1)S(1)} %get-tuple-element.40), channel_id=1, source_target_pairs={{0,4},{1,5},{2,6},{3,7},{4,0},{5,1},{6,2},{7,3},{8,12},{9,13},{10,... | collective-permute-start | bytes 245768 | tf_op jit(solution)/shard_map/ppermute | solution.py:36
  90.1 7.8 %collective-permute-start.21 = (bf16[2,32,640]{2,1,0:T(8,128)(2,1)S(1)}, bf16[2,32,640]{2,1,0:T(8,128)(2,1)S(1)}, u32[]{:S(2)}, u32[]{:S(2)}) collective-permute-start(bf16[2,32,640]{2,1,0:T(8,128)(2,1)S(1)} %get-tuple-element.40), channel_id=1, source_target_pairs={{0,6},{1,7},{2,0},{3,1},{4,2},{5,3},{6,4},{7,5},{8,14},{9,15},{10,... | collective-permute-start | bytes 245768 | tf_op jit(solution)/shard_map/ppermute | solution.py:36
  98.0 1.7 %collective-permute-start.24 = (bf16[2,4,32,640]{3,2,0,1:T(8,128)(2,1)S(1)}, bf16[2,4,32,640]{3,2,0,1:T(8,128)(2,1)S(1)}, u32[]{:S(2)}, u32[]{:S(2)}) collective-permute-start(bf16[2,4,32,640]{3,2,0,1:T(8,128)(2,1)S(1)} %get-tuple-element.31), channel_id=1, source_target_pairs={{0,1},{1,0},{2,3},{3,2},{4,5},{5,4},{6,7},{7,6},{8,9},{9,8},{10,11... | collective-permute-start | bytes 983048 | tf_op jit(solution)/shard_map/ppermute | solution.py:31
  101.7 18.6 %all-to-all-start = ((bf16[32,16,640]{2,1,0:T(8,128)(2,1)}), bf16[32,16,640]{2,1,0:T(8,128)(2,1)S(1)}, u32[]{:S(2)}, u32[]{:S(2)}) async-start(bf16[32,16,640]{2,1,0:T(8,128)(2,1)} %pad_maximum_fusion.3), calls=%async_computation | async-start | bytes 1310720 | tf_op jit(solution)/shard_map/all_to_all | solution.py:197
  122.3 13.4 %all-to-all-start.1 = ((bf16[32,8,512]{2,1,0:T(8,128)(2,1)}), bf16[32,8,512]{2,1,0:T(8,128)(2,1)S(1)}, u32[]{:S(2)}, u32[]{:S(2)}) async-start(bf16[32,8,512]{2,1,0:T(8,128)(2,1)} %copy.46), calls=%async_computation.1 | async-start | bytes 524288 | tf_op jit(solution)/shard_map/all_to_all | solution.py:215
  135.8 1.2 collective-permute-start.25
  137.1 4.6 %collective-permute-start.26 = (f32[8,512]{1,0:T(8,128)S(1)}, f32[8,512]{1,0:T(8,128)S(1)}, u32[]{:S(2)}, u32[]{:S(2)}) collective-permute-start(f32[8,512]{1,0:T(8,128)S(1)} %fusion.112), channel_id=1, source_target_pairs={{0,2},{1,3},{2,0},{3,1},{4,6},{5,7},{6,4},{7,5},{8,10},{9,11},{10,... | collective-permute-start | bytes 49160 | tf_op jit(solution)/shard_map/ppermute | solution.py:121
  141.7 5.8 %collective-permute-start.27 = (f32[8,512]{1,0:T(8,128)S(1)}, f32[8,512]{1,0:T(8,128)S(1)}, u32[]{:S(2)}, u32[]{:S(2)}) collective-permute-start(f32[8,512]{1,0:T(8,128)S(1)} %add.204), channel_id=1, source_target_pairs={{0,6},{1,7},{2,4},{3,5},{4,2},{5,3},{6,0},{7,1},{8,14},{9,15},{10,... | collective-permute-start | bytes 49160 | tf_op jit(solution)/shard_map/ppermute | solution.py:121
  (7 other events, 41.8 us)
